TPU v7x, 256 devices: a whole 4x4x8 slice. The times are simulated.
256 devices in a mesh: seg: 8 (over z), tm: 32 (over y, x, core).
Axes of the slice: x: 4, y: 4, z: 8, core: 2. Of those that a mesh axis runs over, the one named last changes fastest.
Arguments:
- frames: bfloat16 [49152, 1024], P(('seg', 'tm')), parts along dimension 0, may hold values from -6 to 6
- kv_weight: bfloat16 [1024, 256], replicated
- query_weight: bfloat16 [64, 1024, 128], P('tm')
- out_weight: bfloat16 [64, 128, 1024], P('tm'), may hold values from -1.5 to 1.5
- expert_ids: int32 [49152, 4], P(('seg', 'tm')), parts along dimension 0, may hold values from 0 to 63, all different within a row; in each aligned block of 192 rows (0 to 191, 192 to 383, ...) at most 24 rows name the same one
- gate_values: float32 [49152, 4], P(('seg', 'tm')), parts along dimension 0, may hold values from 0.1 to 0.6
Outputs:
- mixed: bfloat16 [49152, 1024], P(('seg', 'tm')), parts along dimension 0
There are 8 independent parts, one for each index of `seg`. A program takes and returns all parts, laid end to end along the dimension named above; an argument that names none is the same for every part. Nothing has to cross between parts.
Inputs may be any that keep to these rules, and one draw needn't show every extreme that they name: `expert_ids`: each row names 4 different experts; within the 192 rows of one device no expert is named more than 24 times, and 24 is reached.
All inputs are finite; a program needn't handle non-finite values.
Results may differ from a plain program's by a relative error of at most 0.011.
Values may be sent and summed in bfloat16 or wider, within the bound.
A program may use at most 64 MiB of HBM per device.

v0:
```python
import math

import jax
import jax.numpy as jnp
from jax import lax
from jax.sharding import PartitionSpec as P


def pick_block(whole_count, largest):
    best_block = 1
    for candidate in range(1, min(whole_count, largest) + 1):
        if whole_count % candidate == 0:
            best_block = candidate
    return best_block


def attend(queries, key_values, head_width):
    row_total = queries.shape[0]
    key_total = key_values.shape[0]
    row_block = pick_block(row_total, 512)
    key_block = pick_block(key_total, 2048)
    scale_factor = 1.0 / math.sqrt(head_width)
    key_tiles = key_values.reshape(key_total // key_block, key_block, 2 * head_width)

    def one_block(query_tile):

        def scores_of(tile):
            raw_scores = lax.dot_general(
                query_tile,
                tile[:, :head_width],
                (((1,), (1,)), ((), ())),
                preferred_element_type=jnp.float32,
            )
            return raw_scores * scale_factor

        def find_peak(peak, tile):
            return (jnp.maximum(peak, jnp.max(scores_of(tile), axis=1)), None)

        start_peak = jnp.full((row_block,), -jnp.inf, jnp.float32)
        peak, _ = lax.scan(find_peak, start_peak, key_tiles)

        def accumulate(state, tile):
            exponent = jnp.exp(scores_of(tile) - peak[:, None])
            new_totals = state[0] + jnp.sum(exponent, axis=1)
            new_summed = state[1] + jnp.dot(
                exponent.astype(jnp.bfloat16),
                tile[:, head_width:],
                preferred_element_type=jnp.float32,
            )
            return ((new_totals, new_summed), None)

        start_state = (
            jnp.zeros((row_block,), jnp.float32),
            jnp.zeros((row_block, head_width), jnp.float32),
        )
        (totals, summed), _ = lax.scan(accumulate, start_state, key_tiles)
        return (summed / totals[:, None]).astype(jnp.bfloat16)

    tiled = queries.reshape(row_total // row_block, row_block, head_width)
    return lax.map(one_block, tiled).reshape(row_total, head_width)


def on_device(frames, kv_weight, query_weight, out_weight, expert_ids, gate_values):
    tok_count = frames.shape[0]
    model_width = frames.shape[1]
    top_count = expert_ids.shape[1]
    local_experts = query_weight.shape[0]
    head_width = query_weight.shape[2]
    owner_count = lax.axis_size("tm")
    expert_count = local_experts * owner_count
    capacity = tok_count * top_count * 2 // expert_count
    local_kv = jnp.dot(frames, kv_weight, preferred_element_type=jnp.float32).astype(jnp.bfloat16)
    key_values = lax.all_gather(local_kv, "tm", axis=0, tiled=True)
    flat_ids = expert_ids.reshape(-1)
    one_hot = (flat_ids[:, None] == jnp.arange(expert_count, dtype=jnp.int32)[None, :]).astype(
        jnp.int32
    )
    earlier = jnp.cumsum(one_hot, axis=0) - one_hot
    position = jnp.sum(earlier * one_hot, axis=1)
    slot_ids = flat_ids * capacity + position
    slot_grid = slot_ids.reshape(tok_count, top_count)
    slot_range = jnp.arange(expert_count * capacity, dtype=jnp.int32)
    chooser = jnp.any(slot_range[:, None, None] == slot_grid[None, :, :], axis=2).astype(
        jnp.bfloat16
    )
    outgoing = jnp.dot(chooser, frames, preferred_element_type=jnp.float32).astype(jnp.bfloat16)
    outgoing = outgoing.reshape(expert_count, capacity, model_width)
    incoming = lax.all_to_all(outgoing, "tm", split_axis=0, concat_axis=0, tiled=True)
    item_count = incoming.shape[1]
    grouped = incoming.reshape(owner_count, local_experts, item_count, model_width)
    queries = jnp.einsum(
        "slid,ldh->lsih", grouped, query_weight, preferred_element_type=jnp.float32
    ).astype(jnp.bfloat16)
    flat_queries = queries.reshape(local_experts * owner_count * item_count, head_width)
    heads = attend(flat_queries, key_values, head_width)
    heads = heads.reshape(local_experts, owner_count, item_count, head_width)
    results = jnp.einsum(
        "lsih,lhd->slid", heads, out_weight, preferred_element_type=jnp.float32
    ).astype(jnp.bfloat16)
    returned = lax.all_to_all(
        results.reshape(expert_count, item_count, model_width),
        "tm",
        split_axis=0,
        concat_axis=0,
        tiled=True,
    )
    flat_back = returned.reshape(expert_count * capacity, model_width)
    picked = flat_back[slot_ids].reshape(tok_count, top_count, model_width)
    mixed = jnp.sum(picked.astype(jnp.float32) * gate_values[:, :, None], axis=1)
    return mixed.astype(jnp.bfloat16)


def solution(mesh):
    placed = (
        P(("seg", "tm"), None),
        P(),
        P("tm", None, None),
        P("tm", None, None),
        P(("seg", "tm"), None),
        P(("seg", "tm"), None),
    )
    return jax.shard_map(
        on_device, mesh=mesh, in_specs=placed, out_specs=P(("seg", "tm"), None), check_vma=False
    )
```

profile of v0, /device:TPU:1, one launch (start us, length us, event | category | flops | bytes accessed | tf_op | source)
XLA Modules:
  0.0 239.0 jit_solution(4295860435194531088)
XLA Ops:
  6.5 2.2 convolution_convert_fusion.1
  8.7 0.8 copy.16
  9.8 1.8 reduce-window.6
  12.2 1.0 fusion.14
  13.3 2.8 %convolution_convert_fusion = bf16[1536,1024]{1,0:T(8,128)(2,1)} fusion(pred[1536,192]{0,1:T(8,128)(4,1)S(1)} %fusion.14, bf16[192,1024]{1,0:T(8,128)(2,1)S(1)} %copy-done.1), kind=kOutput, calls=%fused_computation.23 | convolution fusion | flops 605552640 | bytes 3833856 | tf_op jit(solution)/shard_map/dot_general | solution.py:86
  16.1 8.8 %all-to-all-start = ((bf16[64,24,1024]{2,1,0:T(8,128)(2,1)}), bf16[64,24,1024]{2,1,0:T(8,128)(2,1)}, u32[]{:S(2)}, u32[]{:S(2)}) async-start(bf16[64,24,1024]{2,1,0:T(8,128)(2,1)} %bitcast.68), calls=%async_computation | async-start | bytes 6291456 | tf_op jit(solution)/shard_map/all_to_all | solution.py:88
  24.8 40.0 %all-to-all-done = bf16[64,24,1024]{2,1,0:T(8,128)(2,1)} async-done(((bf16[64,24,1024]{2,1,0:T(8,128)(2,1)}), bf16[64,24,1024]{2,1,0:T(8,128)(2,1)}, u32[]{:S(2)}, u32[]{:S(2)}) %all-to-all-start) | async-done | bytes 3145760 | tf_op jit(solution)/shard_map/all_to_all | solution.py:88
  64.9 2.9 %fusion.17 = bf16[2,32,24,128]{3,2,1,0:T(8,128)(2,1)S(1)} fusion(bf16[32,2,24,1024]{3,2,1,0:T(8,128)(2,1)} %bitcast.4, bf16[2,1024,128]{2,1,0:T(8,128)(2,1)S(1)} %copy-done.3), kind=kOutput, calls=%fused_computation.28 | convolution fusion | flops 402849792 | bytes 4063232 | tf_op jit(solution)/shard_map/slid,ldh->lsih/dot_general | solution.py:91
  67.7 18.6 %all-gather.2.cloned.1.call-done = bf16[6144,256]{1,0:T(8,128)(2,1)} async-done(((bf16[192,256]{1,0:T(8,128)(2,1)}), bf16[6144,256]{1,0:T(8,128)(2,1)}) %all-gather.2.cloned.1.call-update) | async-done | bytes 3145744 | tf_op jit(solution)/shard_map/all_gather | solution.py:73
  86.3 84.6 %while.36 = (s32[]{:T(128)}, bf16[3,512,128]{2,1,0:T(8,128)(2,1)S(1)}, bf16[3,512,128]{2,1,0:T(8,128)(2,1)S(1)}, bf16[3,2048,256]{2,1,0:T(8,128)(2,1)}, s32[]{:T...) while((s32[]{:T(128)}, bf16[3,512,128]{2,1,0:T(8,128)(2,1)S(1)}, ...), condition=%wide.region_11.12_spmd, body=%wide.region_4.11_spmd.sunk | while | flops 813958144 | bytes 15620516 | solution.py:60
  86.3 6.2 %while.37 = (s32[]{:T(128)}, f32[512]{0:T(512)S(1)}, bf16[3,2048,256]{2,1,0:T(8,128)(2,1)}, bf16[512,128]{1,0:T(8,128)(2,1)S(1)}, s32[]{:T(128)}, /*index=5*/s32[]{:T(128)}) while((s32[]{:T(128)}, f32[512]{0:T(512)S(1)}, bf16[3,2048,256]{2,1,0:T(8,128)(2,1)}, bf16[512,128]{1,0:T(8,128)(2,1)S(1)}, s32[]{:T(128)}, ...), condition=%wide.region_7.7_spmd.clone, body=%wide.region_5.6_spmd.clone.sunk | while | flops 270533120 | bytes 2760787 | solution.py:40
  86.4 1.3 dynamic-slice_bitcast_fusion.7
  87.7 0.7 multiply_reduce_fusion.3
  88.4 1.3 dynamic-slice_bitcast_fusion.7
  90.5 1.3 dynamic-slice_bitcast_fusion.7
  92.5 21.8 %while.38 = (s32[]{:T(128)}, f32[512]{0:T(512)S(1)}, f32[512,128]{1,0:T(8,128)S(1)}, bf16[3,2048,256]{2,1,0:T(8,128)(2,1)}, bf16[512,128]{1,0:T(8,128)(2,1)S(1)}, /*index=5*/f32[512]{0:T(512)S(1)}, s32[]{:T(128)}, s32[]{:T(128)}) while((s32[]{:T(128)}, f32[512]{0:T(512)S(1)}, f32[512,128]{1,0:T(8,128)S(1)}, ...), condition=%wide.region_10.10_spmd.clone, body=%wide.region_8.9_spmd.clone.sunk | while | flops 543293952 | bytes 12202084 | solution.py:56
  92.6 1.3 dynamic-slice_bitcast_fusion.8
  93.9 2.8 %fusion.47 = (f32[512]{0:T(512)S(1)}, f32[2048,512]{1,0:T(8,128)}) fusion(f32[512]{0:T(512)S(1)} %get-tuple-element.308, bf16[512,128]{1,0:T(8,128)(2,1)S(1)} %get-tuple-element.307, bf16[2048,256]{1,0:T(8,128)(2,1)S(1)} %dynamic-slice_bitcast_fusion.8), kind=kOutput, calls=%fused_computation.7.clone.1 | convolution fusion | flops 271580672 | bytes 4853760 | tf_op jit(solution)/shard_map/while/body/eval_jaxpr/while/body/eval_jaxpr/dot_general | solution.py:28
  96.7 3.1 %fusion.48 = f32[512,128]{1,0:T(8,128)S(1)} fusion(f32[2048,512]{1,0:T(8,128)} %get-tuple-element.268, f32[512]{0:T(512)S(1)} %get-tuple-element.308, bf16[2048,256]{1,0:T(8,128)(2,1)S(1)} %dynamic-slice_bitcast_fusion.8, f32[512,128]{1,0:T(8,128)S(1)} %get-tuple-element.297, pred[]{:T(512)S(6)} %compare.7), kind=kOutput, calls=%fused_computation.11.clone.1 | convolution fusion | flops 271712256 | bytes 5244929 | tf_op jit(solution)/shard_map/while/body/eval_jaxpr/while/body/eval_jaxpr/dot_general | solution.py:45
  99.8 1.3 dynamic-slice_bitcast_fusion.8
  101.1 2.8 %fusion.47 = (f32[512]{0:T(512)S(1)}, f32[2048,512]{1,0:T(8,128)}) fusion(f32[512]{0:T(512)S(1)} %get-tuple-element.308, bf16[512,128]{1,0:T(8,128)(2,1)S(1)} %get-tuple-element.307, bf16[2048,256]{1,0:T(8,128)(2,1)S(1)} %dynamic-slice_bitcast_fusion.8), kind=kOutput, calls=%fused_computation.7.clone.1 | convolution fusion | flops 271580672 | bytes 4853760 | tf_op jit(solution)/shard_map/while/body/eval_jaxpr/while/body/eval_jaxpr/dot_general | solution.py:28
  103.9 3.1 %fusion.48 = f32[512,128]{1,0:T(8,128)S(1)} fusion(f32[2048,512]{1,0:T(8,128)} %get-tuple-element.268, f32[512]{0:T(512)S(1)} %get-tuple-element.308, bf16[2048,256]{1,0:T(8,128)(2,1)S(1)} %dynamic-slice_bitcast_fusion.8, f32[512,128]{1,0:T(8,128)S(1)} %get-tuple-element.297, pred[]{:T(512)S(6)} %compare.7), kind=kOutput, calls=%fused_computation.11.clone.1 | convolution fusion | flops 271712256 | bytes 5244929 | tf_op jit(solution)/shard_map/while/body/eval_jaxpr/while/body/eval_jaxpr/dot_general | solution.py:45
  107.1 1.3 dynamic-slice_bitcast_fusion.8
  108.4 2.8 %fusion.47 = (f32[512]{0:T(512)S(1)}, f32[2048,512]{1,0:T(8,128)}) fusion(f32[512]{0:T(512)S(1)} %get-tuple-element.308, bf16[512,128]{1,0:T(8,128)(2,1)S(1)} %get-tuple-element.307, bf16[2048,256]{1,0:T(8,128)(2,1)S(1)} %dynamic-slice_bitcast_fusion.8), kind=kOutput, calls=%fused_computation.7.clone.1 | convolution fusion | flops 271580672 | bytes 4853760 | tf_op jit(solution)/shard_map/while/body/eval_jaxpr/while/body/eval_jaxpr/dot_general | solution.py:28
  111.2 3.1 %fusion.48 = f32[512,128]{1,0:T(8,128)S(1)} fusion(f32[2048,512]{1,0:T(8,128)} %get-tuple-element.268, f32[512]{0:T(512)S(1)} %get-tuple-element.308, bf16[2048,256]{1,0:T(8,128)(2,1)S(1)} %dynamic-slice_bitcast_fusion.8, f32[512,128]{1,0:T(8,128)S(1)} %get-tuple-element.297, pred[]{:T(512)S(6)} %compare.7), kind=kOutput, calls=%fused_computation.11.clone.1 | convolution fusion | flops 271712256 | bytes 5244929 | tf_op jit(solution)/shard_map/while/body/eval_jaxpr/while/body/eval_jaxpr/dot_general | solution.py:45
  114.6 6.2 %while.37 = (s32[]{:T(128)}, f32[512]{0:T(512)S(1)}, bf16[3,2048,256]{2,1,0:T(8,128)(2,1)}, bf16[512,128]{1,0:T(8,128)(2,1)S(1)}, s32[]{:T(128)}, /*index=5*/s32[]{:T(128)}) while((s32[]{:T(128)}, f32[512]{0:T(512)S(1)}, bf16[3,2048,256]{2,1,0:T(8,128)(2,1)}, bf16[512,128]{1,0:T(8,128)(2,1)S(1)}, s32[]{:T(128)}, ...), condition=%wide.region_7.7_spmd.clone, body=%wide.region_5.6_spmd.clone.sunk | while | flops 270533120 | bytes 2760787 | solution.py:40
  114.6 1.3 dynamic-slice_bitcast_fusion.7
  115.9 0.7 multiply_reduce_fusion.3
  116.6 1.3 dynamic-slice_bitcast_fusion.7
  118.7 1.3 dynamic-slice_bitcast_fusion.7
  120.0 0.7 multiply_reduce_fusion.3
  120.7 21.8 %while.38 = (s32[]{:T(128)}, f32[512]{0:T(512)S(1)}, f32[512,128]{1,0:T(8,128)S(1)}, bf16[3,2048,256]{2,1,0:T(8,128)(2,1)}, bf16[512,128]{1,0:T(8,128)(2,1)S(1)}, /*index=5*/f32[512]{0:T(512)S(1)}, s32[]{:T(128)}, s32[]{:T(128)}) while((s32[]{:T(128)}, f32[512]{0:T(512)S(1)}, f32[512,128]{1,0:T(8,128)S(1)}, ...), condition=%wide.region_10.10_spmd.clone, body=%wide.region_8.9_spmd.clone.sunk | while | flops 543293952 | bytes 12202084 | solution.py:56
  120.8 1.3 dynamic-slice_bitcast_fusion.8
  122.1 2.8 %fusion.47 = (f32[512]{0:T(512)S(1)}, f32[2048,512]{1,0:T(8,128)}) fusion(f32[512]{0:T(512)S(1)} %get-tuple-element.308, bf16[512,128]{1,0:T(8,128)(2,1)S(1)} %get-tuple-element.307, bf16[2048,256]{1,0:T(8,128)(2,1)S(1)} %dynamic-slice_bitcast_fusion.8), kind=kOutput, calls=%fused_computation.7.clone.1 | convolution fusion | flops 271580672 | bytes 4853760 | tf_op jit(solution)/shard_map/while/body/eval_jaxpr/while/body/eval_jaxpr/dot_general | solution.py:28
  124.9 3.1 %fusion.48 = f32[512,128]{1,0:T(8,128)S(1)} fusion(f32[2048,512]{1,0:T(8,128)} %get-tuple-element.268, f32[512]{0:T(512)S(1)} %get-tuple-element.308, bf16[2048,256]{1,0:T(8,128)(2,1)S(1)} %dynamic-slice_bitcast_fusion.8, f32[512,128]{1,0:T(8,128)S(1)} %get-tuple-element.297, pred[]{:T(512)S(6)} %compare.7), kind=kOutput, calls=%fused_computation.11.clone.1 | convolution fusion | flops 271712256 | bytes 5244929 | tf_op jit(solution)/shard_map/while/body/eval_jaxpr/while/body/eval_jaxpr/dot_general | solution.py:45
  128.0 1.3 dynamic-slice_bitcast_fusion.8
  129.3 2.8 %fusion.47 = (f32[512]{0:T(512)S(1)}, f32[2048,512]{1,0:T(8,128)}) fusion(f32[512]{0:T(512)S(1)} %get-tuple-element.308, bf16[512,128]{1,0:T(8,128)(2,1)S(1)} %get-tuple-element.307, bf16[2048,256]{1,0:T(8,128)(2,1)S(1)} %dynamic-slice_bitcast_fusion.8), kind=kOutput, calls=%fused_computation.7.clone.1 | convolution fusion | flops 271580672 | bytes 4853760 | tf_op jit(solution)/shard_map/while/body/eval_jaxpr/while/body/eval_jaxpr/dot_general | solution.py:28
  132.1 3.1 %fusion.48 = f32[512,128]{1,0:T(8,128)S(1)} fusion(f32[2048,512]{1,0:T(8,128)} %get-tuple-element.268, f32[512]{0:T(512)S(1)} %get-tuple-element.308, bf16[2048,256]{1,0:T(8,128)(2,1)S(1)} %dynamic-slice_bitcast_fusion.8, f32[512,128]{1,0:T(8,128)S(1)} %get-tuple-element.297, pred[]{:T(512)S(6)} %compare.7), kind=kOutput, calls=%fused_computation.11.clone.1 | convolution fusion | flops 271712256 | bytes 5244929 | tf_op jit(solution)/shard_map/while/body/eval_jaxpr/while/body/eval_jaxpr/dot_general | solution.py:45
  135.3 1.3 dynamic-slice_bitcast_fusion.8
  136.6 2.8 %fusion.47 = (f32[512]{0:T(512)S(1)}, f32[2048,512]{1,0:T(8,128)}) fusion(f32[512]{0:T(512)S(1)} %get-tuple-element.308, bf16[512,128]{1,0:T(8,128)(2,1)S(1)} %get-tuple-element.307, bf16[2048,256]{1,0:T(8,128)(2,1)S(1)} %dynamic-slice_bitcast_fusion.8), kind=kOutput, calls=%fused_computation.7.clone.1 | convolution fusion | flops 271580672 | bytes 4853760 | tf_op jit(solution)/shard_map/while/body/eval_jaxpr/while/body/eval_jaxpr/dot_general | solution.py:28
  139.4 3.1 %fusion.48 = f32[512,128]{1,0:T(8,128)S(1)} fusion(f32[2048,512]{1,0:T(8,128)} %get-tuple-element.268, f32[512]{0:T(512)S(1)} %get-tuple-element.308, bf16[2048,256]{1,0:T(8,128)(2,1)S(1)} %dynamic-slice_bitcast_fusion.8, f32[512,128]{1,0:T(8,128)S(1)} %get-tuple-element.297, pred[]{:T(512)S(6)} %compare.7), kind=kOutput, calls=%fused_computation.11.clone.1 | convolution fusion | flops 271712256 | bytes 5244929 | tf_op jit(solution)/shard_map/while/body/eval_jaxpr/while/body/eval_jaxpr/dot_general | solution.py:45
  142.8 6.2 %while.37 = (s32[]{:T(128)}, f32[512]{0:T(512)S(1)}, bf16[3,2048,256]{2,1,0:T(8,128)(2,1)}, bf16[512,128]{1,0:T(8,128)(2,1)S(1)}, s32[]{:T(128)}, /*index=5*/s32[]{:T(128)}) while((s32[]{:T(128)}, f32[512]{0:T(512)S(1)}, bf16[3,2048,256]{2,1,0:T(8,128)(2,1)}, bf16[512,128]{1,0:T(8,128)(2,1)S(1)}, s32[]{:T(128)}, ...), condition=%wide.region_7.7_spmd.clone, body=%wide.region_5.6_spmd.clone.sunk | while | flops 270533120 | bytes 2760787 | solution.py:40
  142.8 1.3 dynamic-slice_bitcast_fusion.7
  144.1 0.7 multiply_reduce_fusion.3
  144.8 1.3 dynamic-slice_bitcast_fusion.7
  146.9 1.3 dynamic-slice_bitcast_fusion.7
  148.2 0.7 multiply_reduce_fusion.3
  149.0 21.8 %while.38 = (s32[]{:T(128)}, f32[512]{0:T(512)S(1)}, f32[512,128]{1,0:T(8,128)S(1)}, bf16[3,2048,256]{2,1,0:T(8,128)(2,1)}, bf16[512,128]{1,0:T(8,128)(2,1)S(1)}, /*index=5*/f32[512]{0:T(512)S(1)}, s32[]{:T(128)}, s32[]{:T(128)}) while((s32[]{:T(128)}, f32[512]{0:T(512)S(1)}, f32[512,128]{1,0:T(8,128)S(1)}, ...), condition=%wide.region_10.10_spmd.clone, body=%wide.region_8.9_spmd.clone.sunk | while | flops 543293952 | bytes 12202084 | solution.py:56
  149.0 1.3 dynamic-slice_bitcast_fusion.8
  150.3 2.8 %fusion.47 = (f32[512]{0:T(512)S(1)}, f32[2048,512]{1,0:T(8,128)}) fusion(f32[512]{0:T(512)S(1)} %get-tuple-element.308, bf16[512,128]{1,0:T(8,128)(2,1)S(1)} %get-tuple-element.307, bf16[2048,256]{1,0:T(8,128)(2,1)S(1)} %dynamic-slice_bitcast_fusion.8), kind=kOutput, calls=%fused_computation.7.clone.1 | convolution fusion | flops 271580672 | bytes 4853760 | tf_op jit(solution)/shard_map/while/body/eval_jaxpr/while/body/eval_jaxpr/dot_general | solution.py:28
  153.1 3.1 %fusion.48 = f32[512,128]{1,0:T(8,128)S(1)} fusion(f32[2048,512]{1,0:T(8,128)} %get-tuple-element.268, f32[512]{0:T(512)S(1)} %get-tuple-element.308, bf16[2048,256]{1,0:T(8,128)(2,1)S(1)} %dynamic-slice_bitcast_fusion.8, f32[512,128]{1,0:T(8,128)S(1)} %get-tuple-element.297, pred[]{:T(512)S(6)} %compare.7), kind=kOutput, calls=%fused_computation.11.clone.1 | convolution fusion | flops 271712256 | bytes 5244929 | tf_op jit(solution)/shard_map/while/body/eval_jaxpr/while/body/eval_jaxpr/dot_general | solution.py:45
  156.2 1.3 dynamic-slice_bitcast_fusion.8
  157.5 2.8 %fusion.47 = (f32[512]{0:T(512)S(1)}, f32[2048,512]{1,0:T(8,128)}) fusion(f32[512]{0:T(512)S(1)} %get-tuple-element.308, bf16[512,128]{1,0:T(8,128)(2,1)S(1)} %get-tuple-element.307, bf16[2048,256]{1,0:T(8,128)(2,1)S(1)} %dynamic-slice_bitcast_fusion.8), kind=kOutput, calls=%fused_computation.7.clone.1 | convolution fusion | flops 271580672 | bytes 4853760 | tf_op jit(solution)/shard_map/while/body/eval_jaxpr/while/body/eval_jaxpr/dot_general | solution.py:28
  160.4 3.1 %fusion.48 = f32[512,128]{1,0:T(8,128)S(1)} fusion(f32[2048,512]{1,0:T(8,128)} %get-tuple-element.268, f32[512]{0:T(512)S(1)} %get-tuple-element.308, bf16[2048,256]{1,0:T(8,128)(2,1)S(1)} %dynamic-slice_bitcast_fusion.8, f32[512,128]{1,0:T(8,128)S(1)} %get-tuple-element.297, pred[]{:T(512)S(6)} %compare.7), kind=kOutput, calls=%fused_computation.11.clone.1 | convolution fusion | flops 271712256 | bytes 5244929 | tf_op jit(solution)/shard_map/while/body/eval_jaxpr/while/body/eval_jaxpr/dot_general | solution.py:45
  163.5 1.3 dynamic-slice_bitcast_fusion.8
  164.8 2.8 %fusion.47 = (f32[512]{0:T(512)S(1)}, f32[2048,512]{1,0:T(8,128)}) fusion(f32[512]{0:T(512)S(1)} %get-tuple-element.308, bf16[512,128]{1,0:T(8,128)(2,1)S(1)} %get-tuple-element.307, bf16[2048,256]{1,0:T(8,128)(2,1)S(1)} %dynamic-slice_bitcast_fusion.8), kind=kOutput, calls=%fused_computation.7.clone.1 | convolution fusion | flops 271580672 | bytes 4853760 | tf_op jit(solution)/shard_map/while/body/eval_jaxpr/while/body/eval_jaxpr/dot_general | solution.py:28
  167.6 3.1 %fusion.48 = f32[512,128]{1,0:T(8,128)S(1)} fusion(f32[2048,512]{1,0:T(8,128)} %get-tuple-element.268, f32[512]{0:T(512)S(1)} %get-tuple-element.308, bf16[2048,256]{1,0:T(8,128)(2,1)S(1)} %dynamic-slice_bitcast_fusion.8, f32[512,128]{1,0:T(8,128)S(1)} %get-tuple-element.297, pred[]{:T(512)S(6)} %compare.7), kind=kOutput, calls=%fused_computation.11.clone.1 | convolution fusion | flops 271712256 | bytes 5244929 | tf_op jit(solution)/shard_map/while/body/eval_jaxpr/while/body/eval_jaxpr/dot_general | solution.py:45
  170.9 1.0 convert_bitcast_fusion
  171.9 2.1 copy.22
  174.1 5.5 %all-to-all-start.1 = ((bf16[64,24,1024]{2,1,0:T(8,128)(2,1)}), bf16[64,24,1024]{2,1,0:T(8,128)(2,1)}, u32[]{:S(2)}, u32[]{:S(2)}) async-start(bf16[64,24,1024]{2,1,0:T(8,128)(2,1)} %bitcast.67), calls=%async_computation.1 | async-start | bytes 6291456 | tf_op jit(solution)/shard_map/all_to_all | solution.py:100
  179.8 38.8 %all-to-all-done.1 = bf16[64,24,1024]{2,1,0:T(8,128)(2,1)} async-done(((bf16[64,24,1024]{2,1,0:T(8,128)(2,1)}), bf16[64,24,1024]{2,1,0:T(8,128)(2,1)}, u32[]{:S(2)}, u32[]{:S(2)}) %all-to-all-start.1) | async-done | bytes 3145760 | tf_op jit(solution)/shard_map/all_to_all | solution.py:100
  218.7 6.1 %gather_fusion = bf16[768,1024]{1,0:T(8,128)(2,1)S(1)} fusion(bf16[1536,1024]{1,0:T(8,128)(2,1)} %bitcast.14, s32[1024]{0:T(1024)S(1)} %pad_clamp_fusion), kind=kCustom, calls=%fused_computation | custom fusion | bytes 3148800 | tf_op jit(solution)/shard_map/gather | solution.py:108
  224.8 2.7 %reshape.79 = f32[192,4,1024]{2,1,0:T(4,128)} reshape(bf16[768,1024]{1,0:T(8,128)(2,1)S(1)} %gather_fusion) | data formatting | bytes 4718592 | tf_op jit(solution)/shard_map/convert_element_type | solution.py:109
  227.4 4.7 %multiply_reduce_fusion.1 = bf16[192,1024]{1,0:T(8,128)(2,1)} fusion(f32[192,4,1024]{2,1,0:T(4,128)} %reshape.79, f32[192,4]{1,0:T(8,128)S(1)} %copy.23), kind=kLoop, calls=%fused_computation.26 | loop fusion | flops 1376256 | bytes 3542016 | tf_op jit(solution)/shard_map/reduce_sum | solution.py:109
  (61 shorter events, 4.8 us)
Async XLA Ops:
  6.5 164.4 %copy-start = (bf16[2,128,1024]{2,1,0:T(8,128)(2,1)S(1)}, bf16[2,128,1024]{2,1,0:T(8,128)(2,1)}, u32[]{:S(2)}) copy-start(bf16[2,128,1024]{2,1,0:T(8,128)(2,1)} %param.15) | copy-start | bytes 1572868
  6.5 6.7 %copy-start.1 = (bf16[192,1024]{1,0:T(8,128)(2,1)S(1)}, bf16[192,1024]{1,0:T(8,128)(2,1)}, u32[]{:S(2)}) copy-start(bf16[192,1024]{1,0:T(8,128)(2,1)} %param.12) | copy-start | bytes 1179652
  6.5 79.8 %all-gather.2.cloned.1.call-start = ((), (), s32[]{:S(2)}) async-start(), calls=%async_computation.2 | async-start | bytes 3244032 | tf_op jit(solution)/shard_map/all_gather | solution.py:73
  16.1 48.8 %copy-start.3 = (bf16[2,1024,128]{2,1,0:T(8,128)(2,1)S(1)}, bf16[2,1024,128]{2,1,0:T(8,128)(2,1)}, u32[]{:S(2)}) copy-start(bf16[2,1024,128]{2,1,0:T(8,128)(2,1)} %param.14) | copy-start | bytes 1572868
  16.1 48.8 %all-to-all-start = ((bf16[64,24,1024]{2,1,0:T(8,128)(2,1)}), bf16[64,24,1024]{2,1,0:T(8,128)(2,1)}, u32[]{:S(2)}, u32[]{:S(2)}) async-start(bf16[64,24,1024]{2,1,0:T(8,128)(2,1)} %bitcast.68), calls=%async_computation | async-start | bytes 6291456 | tf_op jit(solution)/shard_map/all_to_all | solution.py:88
  174.1 5.6 %copy-start.2 = (f32[192,4]{0,1:T(4,128)S(1)}, f32[192,4]{0,1:T(4,128)}, u32[]{:S(2)}) copy-start(f32[192,4]{0,1:T(4,128)} %param.17) | copy-start | bytes 9220
  174.1 44.6 %all-to-all-start.1 = ((bf16[64,24,1024]{2,1,0:T(8,128)(2,1)}), bf16[64,24,1024]{2,1,0:T(8,128)(2,1)}, u32[]{:S(2)}, u32[]{:S(2)}) async-start(bf16[64,24,1024]{2,1,0:T(8,128)(2,1)} %bitcast.67), calls=%async_computation.1 | async-start | bytes 6291456 | tf_op jit(solution)/shard_map/all_to_all | solution.py:100
Sparse Core Ops, SparseCore 0:
  9.9 76.3 all-gather.1
where the time goes:
time: 241 us; the launch traced here: 239 us
  waiting for transfers between devices  97.4 us (40%)
  matrix products  68.6 us (28%)
  local copies, waits for them, and re-layouts  36 us (15%)
  starting transfers between devices  14.2 us (6%)
  between operations  13.6 us (6%)
  other arithmetic  8.5 us (4%)
    all_to_all x1, waiting for transfers between devices, on_device(): lax.all_to_all(outgoing, 'tm', split_axis=0, concat_axis=0, tiled=True)  40 us
    all_to_all x1, waiting for transfers between devices, on_device(): lax.all_to_all(results.reshape(expert_count, item_count, model_width), 't...  38.8 us
    dot_general x18, matrix products, scores_of(): lax.dot_general(query_tile, tile[:, :head_width], (((1,), (1,)), ((), ())...  31.9 us
    dot_general x9, matrix products, accumulate(): jnp.dot(exponent.astype(jnp.bfloat16), tile[:, head_width:], preferred_el...  27.9 us
    squeeze x18, local copies, waits for them, and re-layouts, one_block(): peak, _ = lax.scan(find_peak, start_peak, key_tiles)  23.3 us
    all_gather x1, waiting for transfers between devices, on_device(): key_values = lax.all_gather(local_kv, 'tm', axis=0, tiled=True)  18.6 us
    all_to_all x1, starting transfers between devices, on_device(): lax.all_to_all(outgoing, 'tm', split_axis=0, concat_axis=0, tiled=True)  8.77 us
    gather x1, local copies, waits for them, and re-layouts, on_device(): picked = flat_back[slot_ids].reshape(tok_count, top_count, model_width)  6.11 us
  transfers between devices with their start and end apart: 3, of which 3 were waited for; matrix products, arithmetic and copies ran while one was open for 4% of the time, Pallas kernels for 0%

commit v1 on v0

v1 whole, which is shorter than its diff:
```python
import functools
import math

import jax
import jax.numpy as jnp
from jax import lax
from jax.experimental import pallas as pl
from jax.experimental.pallas import tpu as pltpu
from jax.sharding import PartitionSpec as P

MESH = pl.DeviceIdType.MESH
TOK = 192
D = 1024
HD = 128
CAP = 24
NEXP = 16
SLOTS = NEXP * CAP
KEYS = 6144
N_SEM = 160
BF = jnp.bfloat16
F32 = jnp.float32


def dot(a, b):
    return jnp.dot(a, b, preferred_element_type=F32)


def dot_nt(a, b):
    return lax.dot_general(a, b, (((1,), (1,)), ((), ())), preferred_element_type=F32)


def dot_tn(a, b, precision=None):
    return lax.dot_general(
        a, b, (((0,), (0,)), ((), ())), preferred_element_type=F32, precision=precision
    )


def iota(shape, dim):
    return lax.broadcasted_iota(jnp.int32, shape, dim)


def kernel(
    frames, kvw, qw, ow, ids, gates, out,
    F, R, KV, QW, OW, X, Q, VT, HDS, H, S, GS, PS, RB, send_sem, recv_sem,
):
    z = lax.axis_index("seg")
    t = lax.axis_index("tm")
    c = lax.rem(t, 2)
    x = lax.rem(t // 2, 4)
    y = t // 8

    def dev(dx=0, dy=0, dz=0, dc=0):
        yy = lax.rem(y + dy, 4)
        xx = lax.rem(x + dx, 4)
        return (lax.rem(z + dz, 8), (yy * 4 + xx) * 2 + lax.rem(c + dc, 2))

    sib = dev(dc=1)
    partners = (
        [dev(dx=d) for d in (1, 2, 3)]
        + [dev(dy=d) for d in (1, 2, 3)]
        + [dev(dz=d) for d in (1, 2, 6, 7)]
        + [sib]
    )
    barrier = pltpu.get_barrier_semaphore()
    for p in partners:
        pl.semaphore_signal(barrier, inc=1, device_id=p, device_id_type=MESH)
    pl.semaphore_wait(barrier, len(partners))

    started = []

    def send(src, dst, target):
        n = len(started)
        cp = pltpu.make_async_remote_copy(
            src_ref=src, dst_ref=dst, send_sem=send_sem.at[n], recv_sem=recv_sem.at[n],
            device_id=target, device_id_type=MESH,
        )
        cp.start()
        started.append(cp)
        return cp

    order = (1, 3, 2)
    cp_f = {}
    for d in order:
        cp_f[d] = send(frames, F.at[d], dev(dx=d))
    s4 = lax.rem(z, 4) * 512
    cp_qy = {}
    for d in order:
        cp_qy[d] = send(qw.at[pl.ds(s4, 512)], QW.at[d, pl.ds(s4, 512)], dev(dy=d))
    cp_qs = {0: send(qw, QW.at[4], sib)}

    eye = (iota((TOK, TOK), 0) == iota((TOK, TOK), 1)).astype(F32)
    route = jnp.concatenate([ids[...].astype(F32), gates[...]], axis=1)
    R[0] = dot_tn(route, eye, lax.Precision.HIGHEST)
    cp_r = {d: send(R.at[0], R.at[d], dev(dx=d)) for d in order}

    F[0] = frames[...]
    QW[0] = qw[...]
    OW[0] = ow[...]
    cp_kv = {}
    cp_ks = {}

    def key_values(d):
        rows = pl.ds(d * TOK, TOK)
        KV[rows, :] = dot(F[d], kvw[...]).astype(BF)
        for e in order:
            cp_kv[e, d] = send(KV.at[rows], KV.at[pl.ds((e * 4 + d) * TOK, TOK)], dev(dy=e))
        cp_ks[0, d] = send(KV.at[rows], KV.at[pl.ds((16 + d) * TOK, TOK)], sib)

    key_values(0)

    i16 = iota((NEXP, 1), 0)
    owner = i16 >> 1
    oc = (c + (owner >> 2)) & 1
    oy = (y - (owner & 3)) & 3
    eid = (((oy * 4 + x) * 2 + oc) * 2 + (i16 & 1)).astype(F32)
    ej, ee = iota((SLOTS, NEXP), 0), iota((SLOTS, NEXP), 1) * CAP
    expand = (ej >= ee) & (ej < ee + CAP)
    e_rows = expand.astype(F32).astype(BF)
    i_col = jnp.sum(jnp.where(expand, ej - ee, 0).astype(F32), axis=1, keepdims=True)
    tj, te = iota((NEXP, SLOTS), 1), iota((NEXP, SLOTS), 0) * CAP
    e_cols = ((tj >= te) & (tj < te + CAP)).astype(F32)
    earlier = (iota((TOK, TOK), 0) < iota((TOK, TOK), 1)).astype(F32).astype(BF)

    def select(d):
        r = R[d]
        hit = jnp.zeros((NEXP, TOK), F32)
        gate = jnp.zeros((NEXP, TOK), F32)
        for k in range(4):
            same = r[k:k + 1, :] == eid
            hit = hit + same.astype(F32)
            gate = gate + jnp.where(same, r[4 + k:5 + k, :], 0.0)
        pos = dot(hit.astype(BF), earlier)
        posm = jnp.where(hit > 0.0, pos, -1.0)
        one_hot = (dot(e_rows, posm.astype(BF)) == i_col).astype(F32)
        S[d] = one_hot.astype(BF)
        gate_rows = jnp.dot(
            e_rows.astype(F32), gate, preferred_element_type=F32, precision=lax.Precision.HIGHEST
        )
        GS[pl.ds(d * SLOTS, SLOTS), :] = jnp.broadcast_to(
            jnp.sum(one_hot * gate_rows, axis=1, keepdims=True), (SLOTS, HD)
        )
        picked = dot(S[d], F[d]).astype(BF)
        for p in range(8):
            X[p, d * 48:(d + 1) * 48, :] = picked[p * 48:(p + 1) * 48, :]

    select(0)

    cp_qz = {}
    for e in order:
        cp_qy[e].wait_recv()
        mine = QW.at[e, pl.ds(s4, 512)]
        lo, hi = QW.at[e, pl.ds(s4, 256)], QW.at[e, pl.ds(s4 + 256, 256)]
        cp_qz[e] = [
            send(mine, mine, dev(dz=1)), send(mine, mine, dev(dz=7)),
            send(lo, lo, dev(dz=2)), send(hi, hi, dev(dz=6)),
        ]

    def from_y(e, d):
        cp_kv[e, d].wait_recv()
        rows = pl.ds((e * 4 + d) * TOK, TOK)
        cp_ks[e, d] = send(KV.at[rows], KV.at[pl.ds((16 + e * 4 + d) * TOK, TOK)], sib)

    for d in order:
        cp_f[d].wait_recv()
        key_values(d)
        cp_r[d].wait_recv()
        select(d)

    s2 = lax.rem(z, 2) * 128
    cp_oy = {}
    for e in order:
        cp_oy[e] = send(ow.at[pl.ds(s2, 128)], OW.at[e, pl.ds(s2, 128)], dev(dy=e))
    cp_os = {0: send(ow, OW.at[4], sib)}

    for e in order:
        for d in (0,) + order:
            from_y(e, d)

    row = iota((TOK, 1), 0)
    first = jnp.zeros((TOK, 1), jnp.bool_)
    for b in range(4):
        first = first | ((row >= b * 48) & (row < b * 48 + CAP))

    def project_q(p):
        w = jnp.concatenate([QW[p, 0:D, :], QW[p, D:2 * D, :]], axis=1)
        both = dot(X[p], w)
        q = jnp.where(first, both[:, :HD], both[:, HD:]).astype(BF)
        for b in range(4):
            Q[b * SLOTS + p * 48:b * SLOTS + (p + 1) * 48, :] = q[b * 48:(b + 1) * 48, :]

    project_q(0)
    for e in order:
        for cp in cp_qz[e]:
            cp.wait_recv()
        cp_qs[e] = send(QW.at[e], QW.at[4 + e], sib)
        project_q(e)
    for e in (0,) + order:
        cp_qs[e].wait_recv()
        project_q(4 + e)
    for cp in cp_ks.values():
        cp.wait_recv()

    VT[HD:HD + 16, :] = jnp.ones((16, KEYS), BF)
    CH = 512
    for i in range(KEYS // CH):
        VT[:HD, i * CH:(i + 1) * CH] = KV[i * CH:(i + 1) * CH, HD:].astype(F32).T.astype(BF)

    scale = math.log2(math.e) / math.sqrt(HD)
    RW = 768

    def attend(i):
        base = i * RW
        q = Q[base:base + RW, :]
        m = None
        acc = None
        later = dot_nt(KV[0:CH, :HD], q)
        for n in range(KEYS // CH):
            s = later
            if (n + 1) * CH < KEYS:
                later = dot_nt(KV[(n + 1) * CH:(n + 2) * CH, :HD], q)
            top = jnp.max(s, axis=0, keepdims=True)
            new = top if m is None else jnp.maximum(m, top)
            p = jnp.exp2((s - new) * scale).astype(BF)
            pv = dot(VT[:, n * CH:(n + 1) * CH], p)
            acc = pv if acc is None else acc * jnp.exp2((m - new) * scale) + pv
            m = new
        heads = (acc[:HD] / acc[HD:HD + 1]).T
        HDS[base:base + RW, :] = (heads * GS[base:base + RW, :]).astype(BF)

    attend(0)
    cp_oz = {}
    for e in order:
        cp_oy[e].wait_recv()
        lo, hi = OW.at[e, pl.ds(s2, 64)], OW.at[e, pl.ds(s2 + 64, 64)]
        cp_oz[e] = [send(lo, lo, dev(dz=1)), send(hi, hi, dev(dz=7))]
    attend(1)
    for e in order:
        for cp in cp_oz[e]:
            cp.wait_recv()
        cp_os[e] = send(OW.at[e], OW.at[4 + e], sib)
    for e in (0,) + order:
        cp_os[e].wait_recv()

    half = iota((48, 1), 0) < CAP

    def project_out(b):
        for p in range(8):
            h = HDS[b * SLOTS + p * 48:b * SLOTS + (p + 1) * 48, :].astype(F32)
            pair = jnp.concatenate([jnp.where(half, h, 0.0), jnp.where(half, 0.0, h)], axis=1)
            H[:, p * 256:(p + 1) * 256] = dot_tn(
                S[b, p * 48:(p + 1) * 48, :], pair.astype(BF)
            ).astype(BF)
        return dot(H[...], OW[...].reshape(2048, D))

    cp_back = {}
    for d in (2, 1, 3):
        PS[d - 1] = project_out(d).astype(BF)
        cp_back[d] = send(PS.at[d - 1], RB.at[d - 1], dev(dx=4 - d))
    total = project_out(0)
    for d in (1, 3, 2):
        cp_back[d].wait_recv()
        total = total + RB[d - 1].astype(F32)
    out[...] = total.astype(BF)
    for cp in started:
        cp.wait_send()


def on_device(frames, kv_weight, query_weight, out_weight, expert_ids, gate_values):
    vmem = pl.BlockSpec(memory_space=pltpu.VMEM)
    return pl.pallas_call(
        kernel,
        out_shape=jax.ShapeDtypeStruct((TOK, D), BF),
        in_specs=[vmem] * 6,
        out_specs=vmem,
        scratch_shapes=[
            pltpu.VMEM((4, TOK, D), BF),
            pltpu.VMEM((4, 8, TOK), F32),
            pltpu.VMEM((KEYS, 2 * HD), BF),
            pltpu.VMEM((8, 2 * D, HD), BF),
            pltpu.VMEM((8, 2 * HD, D), BF),
            pltpu.VMEM((8, TOK, D), BF),
            pltpu.VMEM((4 * SLOTS, HD), BF),
            pltpu.VMEM((HD + 16, KEYS), BF),
            pltpu.VMEM((4 * SLOTS, HD), BF),
            pltpu.VMEM((TOK, 2 * D), BF),
            pltpu.VMEM((4, SLOTS, TOK), BF),
            pltpu.VMEM((4 * SLOTS, HD), F32),
            pltpu.VMEM((3, TOK, D), BF),
            pltpu.VMEM((3, TOK, D), BF),
            pltpu.SemaphoreType.DMA((N_SEM,)),
            pltpu.SemaphoreType.DMA((N_SEM,)),
        ],
        compiler_params=pltpu.CompilerParams(
            collective_id=0, has_side_effects=True, vmem_limit_bytes=56 << 20
        ),
        cost_estimate=pl.CostEstimate(
            flops=8_000_000_000, bytes_accessed=4_000_000, transcendentals=9_500_000
        ),
        name="moh",
    )(
        frames,
        kv_weight,
        query_weight.reshape(2 * D, HD),
        out_weight.reshape(2 * HD, D),
        expert_ids,
        gate_values,
    )


def solution(mesh):
    placed = (
        P(("seg", "tm"), None),
        P(),
        P("tm", None, None),
        P("tm", None, None),
        P(("seg", "tm"), None),
        P(("seg", "tm"), None),
    )
    return jax.shard_map(
        on_device, mesh=mesh, in_specs=placed, out_specs=P(("seg", "tm"), None), check_vma=False
    )
```

time: 241 us -> 93.9 us (0.39)
  waiting for transfers between devices: 97.4 us -> 0 us
  Pallas kernels: 0 us -> 89.7 us
  matrix products: 68.6 us -> 0 us
  local copies, waits for them, and re-layouts: 36 us -> 4 us
  starting transfers between devices: 14.2 us -> 0 us
  between operations: 13.6 us -> 0.01 us
  other arithmetic: 8.5 us -> 0 us
    pallas_call x0 -> x1, Pallas kernels: none -> 89.7 us  [on_device(): pl.pallas_call(kernel, out_shape=jax.ShapeDtypeStruct((TOK, D), BF), in_s...]
    all_to_all x2 -> x0, waiting for transfers between devices: 78.8 us -> none  [the longest x1 40 us: on_device(): lax.all_to_all(outgoing, 'tm', split_axis=0, concat_axis=0, tiled=True)]
    dot_general x31 -> x0, matrix products: 68.6 us -> none  [the longest x18 31.9 us: scores_of(): lax.dot_general(query_tile, tile[:, :head_width], (((1,), (1,)), ((), ())...]
    squeeze x21 -> x0, local copies, waits for them, and re-layouts: 23.4 us -> none  [the longest x18 23.3 us: one_block(): peak, _ = lax.scan(find_peak, start_peak, key_tiles)]
    all_gather x1 -> x0, waiting for transfers between devices: 18.6 us -> none  [on_device(): key_values = lax.all_gather(local_kv, 'tm', axis=0, tiled=True)]
    all_to_all x2 -> x0, starting transfers between devices: 14.2 us -> none  [the longest x1 8.77 us: on_device(): lax.all_to_all(outgoing, 'tm', split_axis=0, concat_axis=0, tiled=True)]
    gather x1 -> x0, local copies, waits for them, and re-layouts: 6.11 us -> none  [on_device(): picked = flat_back[slot_ids].reshape(tok_count, top_count, model_width)]
    reduce_sum x2 -> x0, other arithmetic: 4.85 us -> none  [the longest x1 4.71 us: on_device(): jnp.sum(picked.astype(jnp.float32) * gate_values[:, :, None], axis=1)]
  transfers between devices with their start and end apart: 3 -> 0, of which waited for: 3 -> 0; matrix products, arithmetic and copies ran while one was open for 4% -> 0% of each run, Pallas kernels for 0% -> 0%
where the time goes in v1:
time: 93.9 us; the launch traced here: 93.8 us
  Pallas kernels  89.7 us (96%)
  local copies, waits for them, and re-layouts  4 us (4%)
    pallas_call x1, Pallas kernels, on_device(): pl.pallas_call(kernel, out_shape=jax.ShapeDtypeStruct((TOK, D), BF), in_s...  89.7 us
    unnamed x5, local copies, waits for them, and re-layouts  4 us

profile of v1, /device:TPU:1, one launch (start us, length us, event | category | flops | bytes accessed | tf_op | source)
XLA Modules:
  0.0 93.8 jit_solution(508858584624170776)
XLA Ops:
  0.0 0.0 copy-start
  0.0 1.5 %copy.7.ids = s32[192,4]{1,0:T(8,128)} copy(s32[192,4]{0,1:T(4,128)} %param.10) | data formatting | bytes 6144 | tf_op args[4]
  1.5 0.0 copy-done
  1.5 0.8 copy.8.gates
  2.2 89.7 %moh.1 = bf16[192,1024]{1,0:T(8,128)(2,1)} custom-call(bf16[192,1024]{1,0:T(8,128)(2,1)} %frames.1, bf16[1024,256]{1,0:T(8,128)(2,1)} %kvw.1, bf16[2048,128]{1,0:T(8,128)(2,1)} %bitcast.2, bf16[256,1024]{1,0:T(8,128)(2,1)} %bitcast.3, s32[192,4]{1,0:T(8,128)} %copy.7.ids, f32[192,4]{1,0:T(8,128)} %copy.8.gates), custom_call_target="tpu_custom_call" | custom-call | flops 8000000000 | bytes 4000000 | tf_op jit(solution)/shard_map/moh/pallas_call | solution.py:270
  92.0 1.8 %copy.10 = bf16[192,1024]{1,0:T(8,128)(2,1)} copy(bf16[192,1024]{1,0:T(8,128)(2,1)} %moh.1) | data formatting | bytes 786432
Async XLA Ops:
  0.0 1.5 %copy-start = (f32[192,4]{0,1:T(4,128)S(1)}, f32[192,4]{0,1:T(4,128)}, u32[]{:S(2)}) copy-start(f32[192,4]{0,1:T(4,128)} %param.11) | copy-start | bytes 9220

commit v2 on v1

v2 whole, which is shorter than its diff:
```python
import functools
import math

import jax
import jax.numpy as jnp
from jax import lax
from jax.experimental import pallas as pl
from jax.experimental.pallas import tpu as pltpu
from jax.sharding import PartitionSpec as P

MESH = pl.DeviceIdType.MESH
TOK = 192
D = 1024
HD = 128
CAP = 24
NEXP = 16
SLOTS = NEXP * CAP
KEYS = 6144
N_SEM = 96
WC = 512
PLACE = (3, 1, 0, 2)
BF = jnp.bfloat16
F32 = jnp.float32


def dot(a, b):
    return jnp.dot(a, b, preferred_element_type=F32)


def dot_nt(a, b):
    return lax.dot_general(a, b, (((1,), (1,)), ((), ())), preferred_element_type=F32)


def dot_tn(a, b, precision=None):
    return lax.dot_general(
        a, b, (((0,), (0,)), ((), ())), preferred_element_type=F32, precision=precision
    )


def iota(shape, dim):
    return lax.broadcasted_iota(jnp.int32, shape, dim)


def kernel(
    frames, kvw, qw, ow, ids, gates, out,
    F, R, KV, QW, OW, X, Q, VT, HDS, H, S, GS, PS, RB, send_sem, recv_sem,
):
    z = lax.axis_index("seg")
    t = lax.axis_index("tm")
    c = lax.rem(t, 2)
    x = lax.rem(t // 2, 4)
    y = t // 8

    def dev(dx=0, dy=0, dc=0):
        yy = lax.rem(y + dy, 4)
        xx = lax.rem(x + dx, 4)
        return (z, (yy * 4 + xx) * 2 + lax.rem(c + dc, 2))

    sib = dev(dc=1)
    partners = [dev(dx=d) for d in (1, 2, 3)] + [dev(dy=d) for d in (1, 2, 3)] + [sib]
    barrier = pltpu.get_barrier_semaphore()
    for p in partners:
        pl.semaphore_signal(barrier, inc=1, device_id=p, device_id_type=MESH)
    pl.semaphore_wait(barrier, len(partners))

    started = []

    def send(src, dst, target):
        n = len(started)
        cp = pltpu.make_async_remote_copy(
            src_ref=src, dst_ref=dst, send_sem=send_sem.at[n], recv_sem=recv_sem.at[n],
            device_id=target, device_id_type=MESH,
        )
        cp.start()
        started.append(cp)
        return cp

    class Ring:
        def __init__(self, axis, own, slot, size):
            self.up, self.down = dev(**{axis: 1}), dev(**{axis: 3})
            self.slot, h = slot, size // 2
            self.a, self.b = pl.ds(0, h), pl.ds(h, h)
            a, b = own.at[self.a], own.at[self.b]
            self.a1 = send(a, slot(1).at[self.a], self.up)
            self.b3 = send(b, slot(3).at[self.b], self.down)
            self.b1 = send(b, slot(1).at[self.b], self.up)
            self.a3 = send(a, slot(3).at[self.a], self.down)

        def pass_on(self):
            self.a1.wait_recv()
            self.a2 = send(self.slot(1).at[self.a], self.slot(2).at[self.a], self.up)
            self.b3.wait_recv()
            self.b2 = send(self.slot(3).at[self.b], self.slot(2).at[self.b], self.down)

        def wait(self, d):
            for cp in {1: (self.b1,), 3: (self.a3,), 2: (self.a2, self.b2)}[d]:
                cp.wait_recv()

    def kv_at(d, e=0, n=1, sibling=False):
        return KV.at[pl.ds((16 * sibling + d * 4 + e) * TOK, n * TOK)]

    cp_ks = []

    def kv_to_sib(*block):
        cp_ks.append(send(kv_at(*block), kv_at(*block, sibling=True), sib))

    def key_values(d):
        KV[d * 4 * TOK:(d * 4 + 1) * TOK, :] = dot(F[d], kvw[...]).astype(BF)
        kv_to_sib(d)

    order = (1, 3, 2)
    ring_f = Ring("dx", frames, lambda d: F.at[d], TOK)
    R[0, 0:4] = ids[...].astype(F32)
    R[0, 4:8] = gates[...]
    cp_r = {d: send(R.at[0], R.at[d], dev(dx=d)) for d in order}
    F[0] = frames[...]
    key_values(0)
    cp_k = {e: send(kv_at(0), kv_at(0, e), dev(dy=e)) for e in order}
    ring_q = [
        Ring("dy", qw.at[pl.ds(j * D, D)], lambda e, j=j: QW.at[e, pl.ds(j * D, D)], D)
        for j in range(2)
    ]
    cp_qs = [send(qw, QW.at[4], sib)]
    QW[0] = qw[...]
    for j in range(2):
        OW[j, 0] = ow[:, j * WC:(j + 1) * WC]

    i16 = iota((NEXP, 1), 0)
    owner = i16 >> 1
    oc = (c + (owner >> 2)) & 1
    oy = (y - (owner & 3)) & 3
    eid = (((oy * 4 + x) * 2 + oc) * 2 + (i16 & 1)).astype(F32)
    ej, ee = iota((SLOTS, NEXP), 0), iota((SLOTS, NEXP), 1) * CAP
    expand = (ej >= ee) & (ej < ee + CAP)
    e_rows = expand.astype(F32).astype(BF)
    i_col = jnp.sum(jnp.where(expand, ej - ee, 0).astype(F32), axis=1, keepdims=True)
    tj, te = iota((NEXP, SLOTS), 1), iota((NEXP, SLOTS), 0) * CAP
    e_cols = ((tj >= te) & (tj < te + CAP)).astype(F32)
    earlier = (iota((TOK, TOK), 0) < iota((TOK, TOK), 1)).astype(F32).astype(BF)

    def select(d):
        r = R[d]
        hit = jnp.zeros((NEXP, TOK), F32)
        gate = jnp.zeros((NEXP, TOK), F32)
        for k in range(4):
            same = r[k:k + 1, :] == eid
            hit = hit + same.astype(F32)
            gate = gate + jnp.where(same, r[4 + k:5 + k, :], 0.0)
        pos = dot(hit.astype(BF), earlier)
        posm = jnp.where(hit > 0.0, pos, -1.0)
        one_hot = (dot(e_rows, posm.astype(BF)) == i_col).astype(F32)
        S[d] = one_hot.astype(BF)
        gate_rows = jnp.dot(
            e_rows.astype(F32), gate, preferred_element_type=F32, precision=lax.Precision.HIGHEST
        )
        GS[PLACE[d] * SLOTS:(PLACE[d] + 1) * SLOTS, :] = jnp.broadcast_to(
            jnp.sum(one_hot * gate_rows, axis=1, keepdims=True), (SLOTS, HD)
        )
        picked = dot(S[d], F[d]).astype(BF)
        for p in range(8):
            X[p, d * 48:(d + 1) * 48, :] = picked[p * 48:(p + 1) * 48, :]

    select(0)

    ring_f.pass_on()
    for e in order:
        cp_k[e].wait_recv()
    ring_kx = Ring("dx", kv_at(0, 1, 3), lambda d: kv_at(d, 1, 3), 3 * TOK)
    kv_to_sib(0, 1, 3)
    ring_q[0].pass_on()
    for d in (1, 3):
        ring_f.wait(d)
        key_values(d)
        cp_r[d].wait_recv()
        select(d)
    ring_q[1].pass_on()
    ring_o = {}
    cp_os = {}

    def out_weights(j):
        cols = pl.ds(j * WC, WC)
        ring_o[j] = Ring("dy", ow.at[:, cols], lambda e: OW.at[j, e], 2 * HD)
        cp_os[j] = [send(OW.at[j, 0], OW.at[j, 4], sib)]

    out_weights(0)
    ring_f.wait(2)
    key_values(2)
    cp_r[2].wait_recv()
    select(2)
    ring_kx.pass_on()

    row = iota((TOK, 1), 0)
    first = jnp.zeros((TOK, 1), jnp.bool_)
    for b in range(4):
        first = first | ((row >= b * 48) & (row < b * 48 + CAP))

    def project_q(p):
        w = jnp.concatenate([QW[p, 0:D, :], QW[p, D:2 * D, :]], axis=1)
        both = dot(X[p], w)
        q = jnp.where(first, both[:, :HD], both[:, HD:]).astype(BF)
        for b in range(4):
            at = PLACE[b] * SLOTS + p * 48
            Q[at:at + 48, :] = q[b * 48:(b + 1) * 48, :]

    project_q(0)
    for e in (1, 3):
        for ring in ring_q:
            ring.wait(e)
        cp_qs.append(send(QW.at[e], QW.at[4 + e], sib))
        project_q(e)
    for d in (1, 3):
        ring_kx.wait(d)
        kv_to_sib(d, 1, 3)
    for ring in ring_q:
        ring.wait(2)
    cp_qs.append(send(QW.at[2], QW.at[6], sib))
    ring_kx.wait(2)
    kv_to_sib(2, 1, 3)
    project_q(2)
    for e, cp in zip((0,) + order, cp_qs):
        cp.wait_recv()
        project_q(4 + e)
    for cp in cp_ks:
        cp.wait_recv()

    VT[HD:HD + 16, :] = jnp.ones((16, KEYS), BF)
    CH = 512
    for i in range(KEYS // CH):
        VT[:HD, i * CH:(i + 1) * CH] = KV[i * CH:(i + 1) * CH, HD:].astype(F32).T.astype(BF)

    scale = math.log2(math.e) / math.sqrt(HD)
    RW = 768

    def attend(i, between=None):
        base = i * RW
        q = Q[base:base + RW, :]
        m = None
        acc = None
        later = dot_nt(KV[0:CH, :HD], q)
        for n in range(KEYS // CH):
            s = later
            if between is not None and n in between:
                between[n]()
            if (n + 1) * CH < KEYS:
                later = dot_nt(KV[(n + 1) * CH:(n + 2) * CH, :HD], q)
            top = jnp.max(s, axis=0, keepdims=True)
            new = top if m is None else jnp.maximum(m, top)
            p = jnp.exp2((s - new) * scale).astype(BF)
            pv = dot(VT[:, n * CH:(n + 1) * CH], p)
            acc = pv if acc is None else acc * jnp.exp2((m - new) * scale) + pv
            m = new
        heads = (acc[:HD] / acc[HD:HD + 1]).T
        HDS[base:base + RW, :] = (heads * GS[base:base + RW, :]).astype(BF)

    def next_weights():
        ring_o[0].pass_on()
        out_weights(1)

    def all_weights(j):
        for e in order:
            ring_o[j].wait(e)
            cp_os[j].append(send(OW.at[j, e], OW.at[j, 4 + e], sib))
        for cp in cp_os[j]:
            cp.wait_recv()

    half = iota((48, 1), 0) < CAP

    def gather_heads(b):
        for p in range(8):
            at = PLACE[b] * SLOTS + p * 48
            h = HDS[at:at + 48, :].astype(F32)
            pair = jnp.concatenate([jnp.where(half, h, 0.0), jnp.where(half, 0.0, h)], axis=1)
            H[b, :, p * 256:(p + 1) * 256] = dot_tn(
                S[b, p * 48:(p + 1) * 48, :], pair.astype(BF)
            ).astype(BF)

    def project_out(b, j):
        return dot(H[b], OW[j].reshape(2 * D, WC))

    cp_back = {}

    def give_back(d, j):
        PS[j, d - 1] = project_out(d, j).astype(BF)
        cp_back[j, d] = send(PS.at[j, d - 1], RB.at[j, d - 1], dev(dx=4 - d))

    attend(0, {0: next_weights})
    gather_heads(2)
    gather_heads(1)
    all_weights(0)
    give_back(2, 0)
    give_back(1, 0)
    attend(1, {6: lambda: ring_o[1].pass_on()})
    gather_heads(3)
    give_back(3, 0)
    all_weights(1)
    give_back(2, 1)
    give_back(1, 1)
    give_back(3, 1)
    gather_heads(0)
    for j in range(2):
        total = project_out(0, j)
        for d in (2, 1, 3):
            cp_back[j, d].wait_recv()
            total = total + RB[j, d - 1].astype(F32)
        out[:, j * WC:(j + 1) * WC] = total.astype(BF)
    for cp in started:
        cp.wait_send()


def on_device(frames, kv_weight, query_weight, out_weight, expert_ids, gate_values):
    vmem = pl.BlockSpec(memory_space=pltpu.VMEM)
    return pl.pallas_call(
        kernel,
        out_shape=jax.ShapeDtypeStruct((TOK, D), BF),
        in_specs=[vmem] * 6,
        out_specs=vmem,
        scratch_shapes=[
            pltpu.VMEM((4, TOK, D), BF),
            pltpu.VMEM((4, 8, TOK), F32),
            pltpu.VMEM((KEYS, 2 * HD), BF),
            pltpu.VMEM((8, 2 * D, HD), BF),
            pltpu.VMEM((2, 8, 2 * HD, WC), BF),
            pltpu.VMEM((8, TOK, D), BF),
            pltpu.VMEM((4 * SLOTS, HD), BF),
            pltpu.VMEM((HD + 16, KEYS), BF),
            pltpu.VMEM((4 * SLOTS, HD), BF),
            pltpu.VMEM((4, TOK, 2 * D), BF),
            pltpu.VMEM((4, SLOTS, TOK), BF),
            pltpu.VMEM((4 * SLOTS, HD), F32),
            pltpu.VMEM((2, 3, TOK, WC), BF),
            pltpu.VMEM((2, 3, TOK, WC), BF),
            pltpu.SemaphoreType.DMA((N_SEM,)),
            pltpu.SemaphoreType.DMA((N_SEM,)),
        ],
        compiler_params=pltpu.CompilerParams(
            collective_id=0, has_side_effects=True, vmem_limit_bytes=56 << 20
        ),
        cost_estimate=pl.CostEstimate(
            flops=8_000_000_000, bytes_accessed=4_000_000, transcendentals=9_500_000
        ),
        name="moh",
    )(
        frames,
        kv_weight,
        query_weight.reshape(2 * D, HD),
        out_weight.reshape(2 * HD, D),
        expert_ids.T,
        gate_values.T,
    )


def solution(mesh):
    placed = (
        P(("seg", "tm"), None),
        P(),
        P("tm", None, None),
        P("tm", None, None),
        P(("seg", "tm"), None),
        P(("seg", "tm"), None),
    )
    return jax.shard_map(
        on_device, mesh=mesh, in_specs=placed, out_specs=P(("seg", "tm"), None), check_vma=False
    )
```

time: 93.9 us -> 70.7 us (0.75)
  Pallas kernels: 89.7 us -> 68.8 us
  local copies, waits for them, and re-layouts: 4 us -> 1.77 us
    pallas_call x1, Pallas kernels: 89.7 us -> 68.8 us  [on_device(): pl.pallas_call(kernel, out_shape=jax.ShapeDtypeStruct((TOK, D), BF), in_s...]
    unnamed x5 -> x1, local copies, waits for them, and re-layouts: 4 us -> 1.77 us
where the time goes in v2:
time: 70.7 us; the launch traced here: 70.5 us
  Pallas kernels  68.8 us (97%)
  local copies, waits for them, and re-layouts  1.77 us (3%)
    pallas_call x1, Pallas kernels, on_device(): pl.pallas_call(kernel, out_shape=jax.ShapeDtypeStruct((TOK, D), BF), in_s...  68.8 us
    unnamed x1, local copies, waits for them, and re-layouts  1.77 us

profile of v2, /device:TPU:1, one launch (start us, length us, event | category | flops | bytes accessed | tf_op | source)
XLA Modules:
  0.0 70.5 jit_solution(8397850886981248561)
XLA Ops:
  0.0 68.8 %moh.1 = bf16[192,1024]{1,0:T(8,128)(2,1)} custom-call(bf16[192,1024]{1,0:T(8,128)(2,1)} %frames.1, bf16[1024,256]{1,0:T(8,128)(2,1)} %kvw.1, bf16[2048,128]{1,0:T(8,128)(2,1)} %bitcast.4, bf16[256,1024]{1,0:T(8,128)(2,1)} %bitcast.5, s32[4,192]{1,0:T(4,128)} %bitcast.6, f32[4,192]{1,0:T(4,128)} %bitcast.7), custom_call_target="tpu_custom_call" | custom-call | flops 8000000000 | bytes 4000000 | tf_op jit(solution)/shard_map/moh/pallas_call | solution.py:312
  68.8 1.8 %copy.8 = bf16[192,1024]{1,0:T(8,128)(2,1)} copy(bf16[192,1024]{1,0:T(8,128)(2,1)} %moh.1) | data formatting | bytes 786432

commit v3 on v2

--- a/solution.py
+++ b/solution.py
@@ -16,9 +16,12 @@
 NEXP = 16
 SLOTS = NEXP * CAP
 KEYS = 6144
-N_SEM = 96
-WC = 512
-PLACE = (3, 1, 0, 2)
+N_SEM = 128
+NC = 4
+WC = D // NC
+RANK = (0, 2, 6, 4, 1, 3, 7, 5)
+CHUNKS = (0, 4, 1, 3, 5, 7, 2, 6)
+CH = 768
 BF = jnp.bfloat16
 F32 = jnp.float32
 
@@ -35,6 +38,10 @@
     return lax.dot_general(
         a, b, (((0,), (0,)), ((), ())), preferred_element_type=F32, precision=precision
     )
+
+
+def place(p, b):
+    return RANK[p] * 144 + (b - 1) * 48 if b else 1152 + RANK[p] * 48
 
 
 def iota(shape, dim):
@@ -99,30 +106,32 @@
     def kv_at(d, e=0, n=1, sibling=False):
         return KV.at[pl.ds((16 * sibling + d * 4 + e) * TOK, n * TOK)]
 
-    cp_ks = []
+    cp_ks = {}
 
     def kv_to_sib(*block):
-        cp_ks.append(send(kv_at(*block), kv_at(*block, sibling=True), sib))
+        cp_ks[block] = send(kv_at(*block), kv_at(*block, sibling=True), sib)
 
     def key_values(d):
         KV[d * 4 * TOK:(d * 4 + 1) * TOK, :] = dot(F[d], kvw[...]).astype(BF)
         kv_to_sib(d)
 
     order = (1, 3, 2)
+    def query_ring(j):
+        rows = pl.ds(j * D, D)
+        return Ring("dy", qw.at[rows], lambda e: QW.at[e, rows], D)
+
     ring_f = Ring("dx", frames, lambda d: F.at[d], TOK)
+    ring_q = [query_ring(0)]
     R[0, 0:4] = ids[...].astype(F32)
     R[0, 4:8] = gates[...]
     cp_r = {d: send(R.at[0], R.at[d], dev(dx=d)) for d in order}
     F[0] = frames[...]
     key_values(0)
     cp_k = {e: send(kv_at(0), kv_at(0, e), dev(dy=e)) for e in order}
-    ring_q = [
-        Ring("dy", qw.at[pl.ds(j * D, D)], lambda e, j=j: QW.at[e, pl.ds(j * D, D)], D)
-        for j in range(2)
-    ]
+    ring_q.append(query_ring(1))
     cp_qs = [send(qw, QW.at[4], sib)]
     QW[0] = qw[...]
-    for j in range(2):
+    for j in range(NC):
         OW[j, 0] = ow[:, j * WC:(j + 1) * WC]
 
     i16 = iota((NEXP, 1), 0)
@@ -134,8 +143,6 @@
     expand = (ej >= ee) & (ej < ee + CAP)
     e_rows = expand.astype(F32).astype(BF)
     i_col = jnp.sum(jnp.where(expand, ej - ee, 0).astype(F32), axis=1, keepdims=True)
-    tj, te = iota((NEXP, SLOTS), 1), iota((NEXP, SLOTS), 0) * CAP
-    e_cols = ((tj >= te) & (tj < te + CAP)).astype(F32)
     earlier = (iota((TOK, TOK), 0) < iota((TOK, TOK), 1)).astype(F32).astype(BF)
 
     def select(d):
@@ -153,41 +160,55 @@
         gate_rows = jnp.dot(
             e_rows.astype(F32), gate, preferred_element_type=F32, precision=lax.Precision.HIGHEST
         )
-        GS[PLACE[d] * SLOTS:(PLACE[d] + 1) * SLOTS, :] = jnp.broadcast_to(
+        gate_col = jnp.broadcast_to(
             jnp.sum(one_hot * gate_rows, axis=1, keepdims=True), (SLOTS, HD)
         )
         picked = dot(S[d], F[d]).astype(BF)
         for p in range(8):
             X[p, d * 48:(d + 1) * 48, :] = picked[p * 48:(p + 1) * 48, :]
+            GS[place(p, d):place(p, d) + 48, :] = gate_col[p * 48:(p + 1) * 48, :]
 
     select(0)
 
+    ring_q[0].pass_on()
     ring_f.pass_on()
-    for e in order:
-        cp_k[e].wait_recv()
-    ring_kx = Ring("dx", kv_at(0, 1, 3), lambda d: kv_at(d, 1, 3), 3 * TOK)
-    kv_to_sib(0, 1, 3)
-    ring_q[0].pass_on()
     for d in (1, 3):
         ring_f.wait(d)
         key_values(d)
         cp_r[d].wait_recv()
         select(d)
+    for e in order:
+        cp_k[e].wait_recv()
+    ring_kx = Ring("dx", kv_at(0, 1, 3), lambda d: kv_at(d, 1, 3), 3 * TOK)
+    kv_to_sib(0, 1, 3)
     ring_q[1].pass_on()
-    ring_o = {}
-    cp_os = {}
+    ring_o, cp_os = {}, {}
 
     def out_weights(j):
         cols = pl.ds(j * WC, WC)
         ring_o[j] = Ring("dy", ow.at[:, cols], lambda e: OW.at[j, e], 2 * HD)
         cp_os[j] = [send(OW.at[j, 0], OW.at[j, 4], sib)]
 
+    def pass_weights(j):
+        ring_o[j].pass_on()
+        if j + 2 < NC:
+            out_weights(j + 2)
+
+    def relay_weights(j):
+        for e in order:
+            ring_o[j].wait(e)
+            cp_os[j].append(send(OW.at[j, e], OW.at[j, 4 + e], sib))
+
+    def have_weights(j):
+        for cp in cp_os[j]:
+            cp.wait_recv()
+
     out_weights(0)
+    out_weights(1)
     ring_f.wait(2)
     key_values(2)
     cp_r[2].wait_recv()
     select(2)
-    ring_kx.pass_on()
 
     row = iota((TOK, 1), 0)
     first = jnp.zeros((TOK, 1), jnp.bool_)
@@ -198,80 +219,77 @@
         w = jnp.concatenate([QW[p, 0:D, :], QW[p, D:2 * D, :]], axis=1)
         both = dot(X[p], w)
         q = jnp.where(first, both[:, :HD], both[:, HD:]).astype(BF)
-        for b in range(4):
-            at = PLACE[b] * SLOTS + p * 48
-            Q[at:at + 48, :] = q[b * 48:(b + 1) * 48, :]
+        Q[place(p, 0):place(p, 0) + 48, :] = q[:48, :]
+        Q[place(p, 1):place(p, 1) + 144, :] = q[48:, :]
 
     project_q(0)
-    for e in (1, 3):
-        for ring in ring_q:
-            ring.wait(e)
-        cp_qs.append(send(QW.at[e], QW.at[4 + e], sib))
-        project_q(e)
-    for d in (1, 3):
+    cp_qs[0].wait_recv()
+    project_q(4)
+
+    cp_qn = {}
+
+    def sib_keys(d):
+        cp_ks[(d,)].wait_recv()
+        cp_ks[d, 1, 3].wait_recv()
+
+    def column_keys(d):
         ring_kx.wait(d)
         kv_to_sib(d, 1, 3)
-    for ring in ring_q:
-        ring.wait(2)
-    cp_qs.append(send(QW.at[2], QW.at[6], sib))
-    ring_kx.wait(2)
-    kv_to_sib(2, 1, 3)
-    project_q(2)
-    for e, cp in zip((0,) + order, cp_qs):
-        cp.wait_recv()
+
+    def relay_queries(e):
+        for j in range(2):
+            ring_q[j].wait(e)
+            rows = pl.ds(j * D, D)
+            cp_qn[e, j] = send(QW.at[e, rows], QW.at[4 + e, rows], sib)
+
+    relay_queries(1)
+    relay_queries(3)
+    project_q(1)
+    project_q(3)
+    ring_kx.pass_on()
+    for e in (1, 3):
+        cp_qn[e, 0].wait_recv()
+        cp_qn[e, 1].wait_recv()
         project_q(4 + e)
-    for cp in cp_ks:
-        cp.wait_recv()
 
     VT[HD:HD + 16, :] = jnp.ones((16, KEYS), BF)
-    CH = 512
-    for i in range(KEYS // CH):
-        VT[:HD, i * CH:(i + 1) * CH] = KV[i * CH:(i + 1) * CH, HD:].astype(F32).T.astype(BF)
-
     scale = math.log2(math.e) / math.sqrt(HD)
-    RW = 768
-
-    def attend(i, between=None):
-        base = i * RW
-        q = Q[base:base + RW, :]
+
+    def attend(base, size, before):
+        q = Q[base:base + size, :]
+
+        def scores(n):
+            if n in before:
+                before[n]()
+            keys = slice(CHUNKS[n] * CH, (CHUNKS[n] + 1) * CH)
+            if base == 0:
+                VT[:HD, keys] = KV[keys, HD:].astype(F32).T.astype(BF)
+            return dot_nt(KV[keys, :HD], q)
+
         m = None
         acc = None
-        later = dot_nt(KV[0:CH, :HD], q)
-        for n in range(KEYS // CH):
+        later = scores(0)
+        for n in range(len(CHUNKS)):
             s = later
-            if between is not None and n in between:
-                between[n]()
-            if (n + 1) * CH < KEYS:
-                later = dot_nt(KV[(n + 1) * CH:(n + 2) * CH, :HD], q)
+            if n + 1 < len(CHUNKS):
+                later = scores(n + 1)
             top = jnp.max(s, axis=0, keepdims=True)
             new = top if m is None else jnp.maximum(m, top)
             p = jnp.exp2((s - new) * scale).astype(BF)
-            pv = dot(VT[:, n * CH:(n + 1) * CH], p)
+            pv = dot(VT[:, CHUNKS[n] * CH:(CHUNKS[n] + 1) * CH], p)
             acc = pv if acc is None else acc * jnp.exp2((m - new) * scale) + pv
             m = new
         heads = (acc[:HD] / acc[HD:HD + 1]).T
-        HDS[base:base + RW, :] = (heads * GS[base:base + RW, :]).astype(BF)
-
-    def next_weights():
-        ring_o[0].pass_on()
-        out_weights(1)
-
-    def all_weights(j):
-        for e in order:
-            ring_o[j].wait(e)
-            cp_os[j].append(send(OW.at[j, e], OW.at[j, 4 + e], sib))
-        for cp in cp_os[j]:
-            cp.wait_recv()
+        HDS[base:base + size, :] = (heads * GS[base:base + size, :]).astype(BF)
 
     half = iota((48, 1), 0) < CAP
 
     def gather_heads(b):
         for p in range(8):
-            at = PLACE[b] * SLOTS + p * 48
-            h = HDS[at:at + 48, :].astype(F32)
-            pair = jnp.concatenate([jnp.where(half, h, 0.0), jnp.where(half, 0.0, h)], axis=1)
+            h = HDS[place(p, b):place(p, b) + 48, :].astype(F32)
+            both = jnp.concatenate([jnp.where(half, h, 0.0), jnp.where(half, 0.0, h)], axis=1)
             H[b, :, p * 256:(p + 1) * 256] = dot_tn(
-                S[b, p * 48:(p + 1) * 48, :], pair.astype(BF)
+                S[b, p * 48:(p + 1) * 48, :], both.astype(BF)
             ).astype(BF)
 
     def project_out(b, j):
@@ -283,21 +301,43 @@
         PS[j, d - 1] = project_out(d, j).astype(BF)
         cp_back[j, d] = send(PS.at[j, d - 1], RB.at[j, d - 1], dev(dx=4 - d))
 
-    attend(0, {0: next_weights})
-    gather_heads(2)
-    gather_heads(1)
-    all_weights(0)
-    give_back(2, 0)
-    give_back(1, 0)
-    attend(1, {6: lambda: ring_o[1].pass_on()})
-    gather_heads(3)
-    give_back(3, 0)
-    all_weights(1)
-    give_back(2, 1)
-    give_back(1, 1)
-    give_back(3, 1)
+    def give_all(j, *blocks):
+        have_weights(j)
+        for d in blocks:
+            give_back(d, j)
+
+    attend(0, 2 * SLOTS, {
+        1: lambda: sib_keys(0),
+        2: lambda: column_keys(1),
+        3: lambda: column_keys(3),
+        4: lambda: (sib_keys(1), relay_queries(2)),
+        5: lambda: sib_keys(3),
+        6: lambda: (column_keys(2), pass_weights(0)),
+        7: lambda: sib_keys(2),
+    })
+    project_q(2)
+    cp_qn[2, 0].wait_recv()
+    cp_qn[2, 1].wait_recv()
+    project_q(6)
+    attend(2 * SLOTS, SLOTS, {
+        1: lambda: pass_weights(1),
+        6: lambda: relay_weights(0),
+    })
+    for d in (2, 1, 3):
+        gather_heads(d)
+    give_all(0, 2, 1, 3)
+    attend(3 * SLOTS, SLOTS, {
+        1: lambda: pass_weights(2),
+        4: lambda: relay_weights(1),
+        7: lambda: give_all(1, 2, 1, 3),
+    })
+    pass_weights(3)
+    relay_weights(2)
+    give_all(2, 2, 1, 3)
+    relay_weights(3)
+    give_all(3, 2, 1, 3)
     gather_heads(0)
-    for j in range(2):
+    for j in range(NC):
         total = project_out(0, j)
         for d in (2, 1, 3):
             cp_back[j, d].wait_recv()
@@ -319,7 +359,7 @@
             pltpu.VMEM((4, 8, TOK), F32),
             pltpu.VMEM((KEYS, 2 * HD), BF),
             pltpu.VMEM((8, 2 * D, HD), BF),
-            pltpu.VMEM((2, 8, 2 * HD, WC), BF),
+            pltpu.VMEM((NC, 8, 2 * HD, WC), BF),
             pltpu.VMEM((8, TOK, D), BF),
             pltpu.VMEM((4 * SLOTS, HD), BF),
             pltpu.VMEM((HD + 16, KEYS), BF),
@@ -327,8 +367,8 @@
             pltpu.VMEM((4, TOK, 2 * D), BF),
             pltpu.VMEM((4, SLOTS, TOK), BF),
             pltpu.VMEM((4 * SLOTS, HD), F32),
-            pltpu.VMEM((2, 3, TOK, WC), BF),
-            pltpu.VMEM((2, 3, TOK, WC), BF),
+            pltpu.VMEM((NC, 3, TOK, WC), BF),
+            pltpu.VMEM((NC, 3, TOK, WC), BF),
             pltpu.SemaphoreType.DMA((N_SEM,)),
             pltpu.SemaphoreType.DMA((N_SEM,)),
         ],

time: 70.7 us -> 65.8 us (0.931)
  Pallas kernels: 68.8 us -> 63.9 us
    pallas_call x1, Pallas kernels: 68.8 us -> 63.9 us  [on_device(): pl.pallas_call(kernel, out_shape=jax.ShapeDtypeStruct((TOK, D), BF), in_s...]
where the time goes in v3:
time: 65.8 us; the launch traced here: 65.7 us
  Pallas kernels  63.9 us (97%)
  local copies, waits for them, and re-layouts  1.77 us (3%)
    pallas_call x1, Pallas kernels, on_device(): pl.pallas_call(kernel, out_shape=jax.ShapeDtypeStruct((TOK, D), BF), in_s...  63.9 us
    unnamed x1, local copies, waits for them, and re-layouts  1.77 us

profile of v3, /device:TPU:1, one launch (start us, length us, event | category | flops | bytes accessed | tf_op | source)
XLA Modules:
  0.0 65.7 jit_solution(8797655900956799419)
XLA Ops:
  0.0 63.9 %moh.1 = bf16[192,1024]{1,0:T(8,128)(2,1)} custom-call(bf16[192,1024]{1,0:T(8,128)(2,1)} %frames.1, bf16[1024,256]{1,0:T(8,128)(2,1)} %kvw.1, bf16[2048,128]{1,0:T(8,128)(2,1)} %bitcast.4, bf16[256,1024]{1,0:T(8,128)(2,1)} %bitcast.5, s32[4,192]{1,0:T(4,128)} %bitcast.6, f32[4,192]{1,0:T(4,128)} %bitcast.7), custom_call_target="tpu_custom_call" | custom-call | flops 8000000000 | bytes 4000000 | tf_op jit(solution)/shard_map/moh/pallas_call | solution.py:352
  63.9 1.8 %copy.8 = bf16[192,1024]{1,0:T(8,128)(2,1)} copy(bf16[192,1024]{1,0:T(8,128)(2,1)} %moh.1) | data formatting | bytes 786432

commit v4 on v3

--- a/solution.py
+++ b/solution.py
@@ -49,8 +49,8 @@
 
 
 def kernel(
-    frames, kvw, qw, ow, ids, gates, out,
-    F, R, KV, QW, OW, X, Q, VT, HDS, H, S, GS, PS, RB, send_sem, recv_sem,
+    frames_in, kvw_in, qw_in, ow_in, ids_in, gates_in, out,
+    F, R, KV, QW, OW, X, Q, VT, HDS, H, S, GS, PS, PF, TB, RB, OWN, kvw, ids, gates, send_sem, recv_sem, keep_sem,
 ):
     z = lax.axis_index("seg")
     t = lax.axis_index("tm")
@@ -65,11 +65,22 @@
 
     sib = dev(dc=1)
     partners = [dev(dx=d) for d in (1, 2, 3)] + [dev(dy=d) for d in (1, 2, 3)] + [sib]
+    frames, qw, ow = F.at[0], QW.at[0], OWN
+    kept = [
+        pltpu.make_async_copy(src, dst, keep_sem.at[n])
+        for n, (src, dst) in enumerate((
+            (frames_in, frames), (kvw_in, kvw), (ids_in, ids), (gates_in, gates), (qw_in, qw), (ow_in, ow),
+        ))
+    ]
+    for cp in kept:
+        cp.start()
     barrier = pltpu.get_barrier_semaphore()
     for p in partners:
         pl.semaphore_signal(barrier, inc=1, device_id=p, device_id_type=MESH)
     pl.semaphore_wait(barrier, len(partners))
 
+    for cp in kept:
+        cp.wait()
     started = []
 
     def send(src, dst, target):
@@ -125,12 +136,10 @@
     R[0, 0:4] = ids[...].astype(F32)
     R[0, 4:8] = gates[...]
     cp_r = {d: send(R.at[0], R.at[d], dev(dx=d)) for d in order}
-    F[0] = frames[...]
     key_values(0)
     cp_k = {e: send(kv_at(0), kv_at(0, e), dev(dy=e)) for e in order}
     ring_q.append(query_ring(1))
     cp_qs = [send(qw, QW.at[4], sib)]
-    QW[0] = qw[...]
     for j in range(NC):
         OW[j, 0] = ow[:, j * WC:(j + 1) * WC]
 
@@ -295,16 +304,37 @@
     def project_out(b, j):
         return dot(H[b], OW[j].reshape(2 * D, WC))
 
-    cp_back = {}
-
-    def give_back(d, j):
-        PS[j, d - 1] = project_out(d, j).astype(BF)
-        cp_back[j, d] = send(PS.at[j, d - 1], RB.at[j, d - 1], dev(dx=4 - d))
-
-    def give_all(j, *blocks):
+    cp_back, cp_via = {}, {}
+    halves = (pl.ds(0, TOK // 2), pl.ds(TOK // 2, TOK // 2))
+    ends = (dev(dx=3), dev(dx=1))
+
+    def give_far(j):
+        PS[j, 2] = project_out(2, j).astype(BF)
+        for k in (0, 1):
+            cp_via[j, k] = send(PS.at[j, 2, halves[1 - k]], TB.at[j, k], ends[k])
+
+    def give_half(j, k, h):
+        cp_back[j, k, h] = send(PS.at[j, k, halves[h]], RB.at[j, k, halves[h]], ends[k])
+
+    def give_near(j, k):
+        part = project_out(1 + 2 * k, j)
+        late, n = 1 - k, TOK // 2
+        PS[j, k, k * n:(k + 1) * n, :] = part[k * n:(k + 1) * n, :].astype(BF)
+        PF[j, k] = part[late * n:(late + 1) * n, :]
+        give_half(j, k, k)
+
+    def finish(j):
+        for k in (0, 1):
+            late, n = 1 - k, TOK // 2
+            cp_via[j, k].wait_recv()
+            PS[j, k, late * n:(late + 1) * n, :] = (PF[j, k] + TB[j, k].astype(F32)).astype(BF)
+            give_half(j, k, late)
+
+    def give_all(j):
         have_weights(j)
-        for d in blocks:
-            give_back(d, j)
+        give_far(j)
+        give_near(j, 0)
+        give_near(j, 1)
 
     attend(0, 2 * SLOTS, {
         1: lambda: sib_keys(0),
@@ -325,34 +355,42 @@
     })
     for d in (2, 1, 3):
         gather_heads(d)
-    give_all(0, 2, 1, 3)
+    give_all(0)
     attend(3 * SLOTS, SLOTS, {
         1: lambda: pass_weights(2),
-        4: lambda: relay_weights(1),
-        7: lambda: give_all(1, 2, 1, 3),
+        3: lambda: (relay_weights(1), pass_weights(3)),
+        5: lambda: give_all(1),
+        7: lambda: (finish(0), relay_weights(2)),
     })
-    pass_weights(3)
-    relay_weights(2)
-    give_all(2, 2, 1, 3)
+    gather_heads(0)
+    own = {}
+    give_all(2)
     relay_weights(3)
-    give_all(3, 2, 1, 3)
-    gather_heads(0)
+    own[0] = project_out(0, 0)
+    finish(1)
+    own[1] = project_out(0, 1)
+    give_all(3)
+    own[2] = project_out(0, 2)
+    own[3] = project_out(0, 3)
+    finish(2)
+    finish(3)
     for j in range(NC):
-        total = project_out(0, j)
-        for d in (2, 1, 3):
-            cp_back[j, d].wait_recv()
-            total = total + RB[j, d - 1].astype(F32)
+        total = own[j]
+        for k in (0, 1):
+            cp_back[j, k, 0].wait_recv()
+            cp_back[j, k, 1].wait_recv()
+            total = total + RB[j, k].astype(F32)
         out[:, j * WC:(j + 1) * WC] = total.astype(BF)
     for cp in started:
         cp.wait_send()
 
 
 def on_device(frames, kv_weight, query_weight, out_weight, expert_ids, gate_values):
-    vmem = pl.BlockSpec(memory_space=pltpu.VMEM)
+    vmem, hbm = pl.BlockSpec(memory_space=pltpu.VMEM), pl.BlockSpec(memory_space=pltpu.HBM)
     return pl.pallas_call(
         kernel,
-        out_shape=jax.ShapeDtypeStruct((TOK, D), BF),
-        in_specs=[vmem] * 6,
+        out_shape=pltpu.VMEM((TOK, D), BF),
+        in_specs=[hbm] * 6,
         out_specs=vmem,
         scratch_shapes=[
             pltpu.VMEM((4, TOK, D), BF),
@@ -368,9 +406,16 @@
             pltpu.VMEM((4, SLOTS, TOK), BF),
             pltpu.VMEM((4 * SLOTS, HD), F32),
             pltpu.VMEM((NC, 3, TOK, WC), BF),
-            pltpu.VMEM((NC, 3, TOK, WC), BF),
+            pltpu.VMEM((NC, 2, TOK // 2, WC), F32),
+            pltpu.VMEM((NC, 2, TOK // 2, WC), BF),
+            pltpu.VMEM((NC, 2, TOK, WC), BF),
+            pltpu.VMEM((2 * HD, D), BF),
+            pltpu.VMEM((D, 2 * HD), BF),
+            pltpu.VMEM((4, TOK), jnp.int32),
+            pltpu.VMEM((4, TOK), F32),
             pltpu.SemaphoreType.DMA((N_SEM,)),
             pltpu.SemaphoreType.DMA((N_SEM,)),
+            pltpu.SemaphoreType.DMA((6,)),
         ],
         compiler_params=pltpu.CompilerParams(
             collective_id=0, has_side_effects=True, vmem_limit_bytes=56 << 20

time: 65.8 us -> 61.4 us (0.933)
  Pallas kernels: 63.9 us -> 60.1 us
  local copies, waits for them, and re-layouts: 1.77 us -> 0.75 us
    pallas_call x1, Pallas kernels: 63.9 us -> 60.1 us  [on_device(): pl.pallas_call(kernel, out_shape=pltpu.VMEM((TOK, D), BF), in_specs=[hbm]...]
    unnamed x1, local copies, waits for them, and re-layouts: 1.77 us -> 0.75 us
where the time goes in v4:
time: 61.4 us; the launch traced here: 60.9 us
  Pallas kernels  60.1 us (98%)
  local copies, waits for them, and re-layouts  0.75 us (1%)
    pallas_call x1, Pallas kernels, on_device(): pl.pallas_call(kernel, out_shape=pltpu.VMEM((TOK, D), BF), in_specs=[hbm]...  60.1 us

profile of v4, /device:TPU:1, one launch (start us, length us, event | category | flops | bytes accessed | tf_op | source)
XLA Modules:
  0.0 60.9 jit_solution(16075902525684254288)
XLA Ops:
  0.0 60.1 %moh.1 = bf16[192,1024]{1,0:T(8,128)(2,1)S(1)} custom-call(bf16[192,1024]{1,0:T(8,128)(2,1)} %frames_in.1, bf16[1024,256]{1,0:T(8,128)(2,1)} %kvw_in.1, bf16[2048,128]{1,0:T(8,128)(2,1)} %bitcast.4, bf16[256,1024]{1,0:T(8,128)(2,1)} %bitcast.5, s32[4,192]{1,0:T(4,128)} %bitcast.6, f32[4,192]{1,0:T(4,128)} %bitcast.7), custom_call_target="tpu_custom_call" | custom-call | flops 8000000000 | bytes 4000000 | tf_op jit(solution)/shard_map/moh/pallas_call | solution.py:390
  60.2 0.7 %copy.8 = bf16[192,1024]{1,0:T(8,128)(2,1)} copy(bf16[192,1024]{1,0:T(8,128)(2,1)S(1)} %moh.1) | data formatting | bytes 786432

commit v5 on v4

--- a/solution.py
+++ b/solution.py
@@ -17,8 +17,9 @@
 SLOTS = NEXP * CAP
 KEYS = 6144
 N_SEM = 128
-NC = 4
-WC = D // NC
+CUTS = (0, 512, 768, 1024)
+WIDTHS = (512, 256, 256)
+NC = len(WIDTHS)
 RANK = (0, 2, 6, 4, 1, 3, 7, 5)
 CHUNKS = (0, 4, 1, 3, 5, 7, 2, 6)
 CH = 768
@@ -132,16 +133,15 @@
         return Ring("dy", qw.at[rows], lambda e: QW.at[e, rows], D)
 
     ring_f = Ring("dx", frames, lambda d: F.at[d], TOK)
-    ring_q = [query_ring(0)]
     R[0, 0:4] = ids[...].astype(F32)
     R[0, 4:8] = gates[...]
     cp_r = {d: send(R.at[0], R.at[d], dev(dx=d)) for d in order}
     key_values(0)
-    cp_k = {e: send(kv_at(0), kv_at(0, e), dev(dy=e)) for e in order}
-    ring_q.append(query_ring(1))
+    ring_k = Ring("dy", kv_at(0), lambda e: kv_at(0, e), TOK)
+    ring_q = [query_ring(0)]
     cp_qs = [send(qw, QW.at[4], sib)]
     for j in range(NC):
-        OW[j, 0] = ow[:, j * WC:(j + 1) * WC]
+        OW[j][0] = ow[:, CUTS[j]:CUTS[j + 1]]
 
     i16 = iota((NEXP, 1), 0)
     owner = i16 >> 1
@@ -179,41 +179,40 @@
 
     select(0)
 
+    ring_k.pass_on()
+    ring_q.append(query_ring(1))
+    ring_f.pass_on()
     ring_q[0].pass_on()
-    ring_f.pass_on()
     for d in (1, 3):
         ring_f.wait(d)
         key_values(d)
         cp_r[d].wait_recv()
         select(d)
     for e in order:
-        cp_k[e].wait_recv()
+        ring_k.wait(e)
     ring_kx = Ring("dx", kv_at(0, 1, 3), lambda d: kv_at(d, 1, 3), 3 * TOK)
     kv_to_sib(0, 1, 3)
     ring_q[1].pass_on()
     ring_o, cp_os = {}, {}
 
     def out_weights(j):
-        cols = pl.ds(j * WC, WC)
-        ring_o[j] = Ring("dy", ow.at[:, cols], lambda e: OW.at[j, e], 2 * HD)
-        cp_os[j] = [send(OW.at[j, 0], OW.at[j, 4], sib)]
+        cols = pl.ds(CUTS[j], WIDTHS[j])
+        ring_o[j] = Ring("dy", ow.at[:, cols], lambda e: OW[j].at[e], 2 * HD)
+        cp_os[j] = [send(OW[j].at[0], OW[j].at[4], sib)]
 
     def pass_weights(j):
         ring_o[j].pass_on()
-        if j + 2 < NC:
-            out_weights(j + 2)
 
     def relay_weights(j):
         for e in order:
             ring_o[j].wait(e)
-            cp_os[j].append(send(OW.at[j, e], OW.at[j, 4 + e], sib))
+            cp_os[j].append(send(OW[j].at[e], OW[j].at[4 + e], sib))
 
     def have_weights(j):
         for cp in cp_os[j]:
             cp.wait_recv()
 
     out_weights(0)
-    out_weights(1)
     ring_f.wait(2)
     key_values(2)
     cp_r[2].wait_recv()
@@ -302,32 +301,32 @@
             ).astype(BF)
 
     def project_out(b, j):
-        return dot(H[b], OW[j].reshape(2 * D, WC))
+        return dot(H[b], OW[j][...].reshape(2 * D, WIDTHS[j]))
 
     cp_back, cp_via = {}, {}
     halves = (pl.ds(0, TOK // 2), pl.ds(TOK // 2, TOK // 2))
     ends = (dev(dx=3), dev(dx=1))
 
     def give_far(j):
-        PS[j, 2] = project_out(2, j).astype(BF)
+        PS[j][2] = project_out(2, j).astype(BF)
         for k in (0, 1):
-            cp_via[j, k] = send(PS.at[j, 2, halves[1 - k]], TB.at[j, k], ends[k])
+            cp_via[j, k] = send(PS[j].at[2, halves[1 - k]], TB[j].at[k], ends[k])
 
     def give_half(j, k, h):
-        cp_back[j, k, h] = send(PS.at[j, k, halves[h]], RB.at[j, k, halves[h]], ends[k])
+        cp_back[j, k, h] = send(PS[j].at[k, halves[h]], RB[j].at[k, halves[h]], ends[k])
 
     def give_near(j, k):
         part = project_out(1 + 2 * k, j)
         late, n = 1 - k, TOK // 2
-        PS[j, k, k * n:(k + 1) * n, :] = part[k * n:(k + 1) * n, :].astype(BF)
-        PF[j, k] = part[late * n:(late + 1) * n, :]
+        PS[j][k, k * n:(k + 1) * n, :] = part[k * n:(k + 1) * n, :].astype(BF)
+        PF[j][k] = part[late * n:(late + 1) * n, :]
         give_half(j, k, k)
 
     def finish(j):
         for k in (0, 1):
             late, n = 1 - k, TOK // 2
             cp_via[j, k].wait_recv()
-            PS[j, k, late * n:(late + 1) * n, :] = (PF[j, k] + TB[j, k].astype(F32)).astype(BF)
+            PS[j][k, late * n:(late + 1) * n, :] = (PF[j][k] + TB[j][k].astype(F32)).astype(BF)
             give_half(j, k, late)
 
     def give_all(j):
@@ -342,45 +341,47 @@
         3: lambda: column_keys(3),
         4: lambda: (sib_keys(1), relay_queries(2)),
         5: lambda: sib_keys(3),
-        6: lambda: (column_keys(2), pass_weights(0)),
-        7: lambda: sib_keys(2),
+        6: lambda: column_keys(2),
+        7: lambda: (sib_keys(2), pass_weights(0), out_weights(1), out_weights(2)),
     })
     project_q(2)
     cp_qn[2, 0].wait_recv()
     cp_qn[2, 1].wait_recv()
     project_q(6)
     attend(2 * SLOTS, SLOTS, {
-        1: lambda: pass_weights(1),
-        6: lambda: relay_weights(0),
+        7: lambda: relay_weights(0),
     })
     for d in (2, 1, 3):
         gather_heads(d)
     give_all(0)
     attend(3 * SLOTS, SLOTS, {
-        1: lambda: pass_weights(2),
-        3: lambda: (relay_weights(1), pass_weights(3)),
-        5: lambda: give_all(1),
-        7: lambda: (finish(0), relay_weights(2)),
+        2: lambda: pass_weights(1),
+        6: lambda: pass_weights(2),
     })
     gather_heads(0)
-    own = {}
-    give_all(2)
-    relay_weights(3)
-    own[0] = project_out(0, 0)
+    finish(0)
+    relay_weights(1)
+    own = {0: project_out(0, 0)}
+    have_weights(1)
+    give_far(1)
+    relay_weights(2)
+    give_near(1, 0)
+    give_near(1, 1)
+    have_weights(2)
+    give_far(2)
+    give_near(2, 0)
+    give_near(2, 1)
+    own[1] = project_out(0, 1)
+    own[2] = project_out(0, 2)
     finish(1)
-    own[1] = project_out(0, 1)
-    give_all(3)
-    own[2] = project_out(0, 2)
-    own[3] = project_out(0, 3)
     finish(2)
-    finish(3)
     for j in range(NC):
         total = own[j]
         for k in (0, 1):
             cp_back[j, k, 0].wait_recv()
             cp_back[j, k, 1].wait_recv()
-            total = total + RB[j, k].astype(F32)
-        out[:, j * WC:(j + 1) * WC] = total.astype(BF)
+            total = total + RB[j][k].astype(F32)
+        out[:, CUTS[j]:CUTS[j + 1]] = total.astype(BF)
     for cp in started:
         cp.wait_send()
 
@@ -397,7 +398,7 @@
             pltpu.VMEM((4, 8, TOK), F32),
             pltpu.VMEM((KEYS, 2 * HD), BF),
             pltpu.VMEM((8, 2 * D, HD), BF),
-            pltpu.VMEM((NC, 8, 2 * HD, WC), BF),
+            [pltpu.VMEM((8, 2 * HD, w), BF) for w in WIDTHS],
             pltpu.VMEM((8, TOK, D), BF),
             pltpu.VMEM((4 * SLOTS, HD), BF),
             pltpu.VMEM((HD + 16, KEYS), BF),
@@ -405,10 +406,10 @@
             pltpu.VMEM((4, TOK, 2 * D), BF),
             pltpu.VMEM((4, SLOTS, TOK), BF),
             pltpu.VMEM((4 * SLOTS, HD), F32),
-            pltpu.VMEM((NC, 3, TOK, WC), BF),
-            pltpu.VMEM((NC, 2, TOK // 2, WC), F32),
-            pltpu.VMEM((NC, 2, TOK // 2, WC), BF),
-            pltpu.VMEM((NC, 2, TOK, WC), BF),
+            [pltpu.VMEM((3, TOK, w), BF) for w in WIDTHS],
+            [pltpu.VMEM((2, TOK // 2, w), F32) for w in WIDTHS],
+            [pltpu.VMEM((2, TOK // 2, w), BF) for w in WIDTHS],
+            [pltpu.VMEM((2, TOK, w), BF) for w in WIDTHS],
             pltpu.VMEM((2 * HD, D), BF),
             pltpu.VMEM((D, 2 * HD), BF),
             pltpu.VMEM((4, TOK), jnp.int32),

time: 61.4 us -> 60.3 us (0.982); the launches traced: 60.9 us -> 59.1 us
  Pallas kernels: 60.1 us -> 58.4 us
    pallas_call x1, Pallas kernels: 60.1 us -> 58.4 us  [on_device(): pl.pallas_call(kernel, out_shape=pltpu.VMEM((TOK, D), BF), in_specs=[hbm]...]
where the time goes in v5:
time: 60.3 us; the launch traced here: 59.1 us
  Pallas kernels  58.4 us (97%)
  local copies, waits for them, and re-layouts  0.75 us (1%)
    pallas_call x1, Pallas kernels, on_device(): pl.pallas_call(kernel, out_shape=pltpu.VMEM((TOK, D), BF), in_specs=[hbm]...  58.4 us

profile of v5, /device:TPU:1, one launch (start us, length us, event | category | flops | bytes accessed | tf_op | source)
XLA Modules:
  0.0 59.1 jit_solution(7759474575318830933)
XLA Ops:
  0.0 58.4 %moh.1 = bf16[192,1024]{1,0:T(8,128)(2,1)S(1)} custom-call(bf16[192,1024]{1,0:T(8,128)(2,1)} %frames_in.1, bf16[1024,256]{1,0:T(8,128)(2,1)} %kvw_in.1, bf16[2048,128]{1,0:T(8,128)(2,1)} %bitcast.4, bf16[256,1024]{1,0:T(8,128)(2,1)} %bitcast.5, s32[4,192]{1,0:T(4,128)} %bitcast.6, f32[4,192]{1,0:T(4,128)} %bitcast.7), custom_call_target="tpu_custom_call" | custom-call | flops 8000000000 | bytes 4000000 | tf_op jit(solution)/shard_map/moh/pallas_call | solution.py:391
  58.4 0.7 %copy.8 = bf16[192,1024]{1,0:T(8,128)(2,1)} copy(bf16[192,1024]{1,0:T(8,128)(2,1)S(1)} %moh.1) | data formatting | bytes 786432

commit v6 on v5

--- a/solution.py
+++ b/solution.py
@@ -80,8 +80,6 @@
         pl.semaphore_signal(barrier, inc=1, device_id=p, device_id_type=MESH)
     pl.semaphore_wait(barrier, len(partners))
 
-    for cp in kept:
-        cp.wait()
     started = []
 
     def send(src, dst, target):
@@ -132,14 +130,20 @@
         rows = pl.ds(j * D, D)
         return Ring("dy", qw.at[rows], lambda e: QW.at[e, rows], D)
 
+    kept[0].wait()
     ring_f = Ring("dx", frames, lambda d: F.at[d], TOK)
+    kept[2].wait()
+    kept[3].wait()
     R[0, 0:4] = ids[...].astype(F32)
     R[0, 4:8] = gates[...]
     cp_r = {d: send(R.at[0], R.at[d], dev(dx=d)) for d in order}
+    kept[1].wait()
     key_values(0)
     ring_k = Ring("dy", kv_at(0), lambda e: kv_at(0, e), TOK)
+    kept[4].wait()
     ring_q = [query_ring(0)]
     cp_qs = [send(qw, QW.at[4], sib)]
+    kept[5].wait()
     for j in range(NC):
         OW[j][0] = ow[:, CUTS[j]:CUTS[j + 1]]
 

time: 60.3 us -> 60.3 us (level)
  no operation moved by 1% of the time
where the time goes in v6:
time: 60.3 us; the launch traced here: 59.1 us
  Pallas kernels  58.4 us (97%)
  local copies, waits for them, and re-layouts  0.75 us (1%)
    pallas_call x1, Pallas kernels, on_device(): pl.pallas_call(kernel, out_shape=pltpu.VMEM((TOK, D), BF), in_specs=[hbm]...  58.4 us

profile of v6, /device:TPU:1, one launch (start us, length us, event | category | flops | bytes accessed | tf_op | source)
XLA Modules:
  0.0 59.1 jit_solution(1671163101072092776)
XLA Ops:
  0.0 58.4 %moh.1 = bf16[192,1024]{1,0:T(8,128)(2,1)S(1)} custom-call(bf16[192,1024]{1,0:T(8,128)(2,1)} %frames_in.1, bf16[1024,256]{1,0:T(8,128)(2,1)} %kvw_in.1, bf16[2048,128]{1,0:T(8,128)(2,1)} %bitcast.4, bf16[256,1024]{1,0:T(8,128)(2,1)} %bitcast.5, s32[4,192]{1,0:T(4,128)} %bitcast.6, f32[4,192]{1,0:T(4,128)} %bitcast.7), custom_call_target="tpu_custom_call" | custom-call | flops 8000000000 | bytes 4000000 | tf_op jit(solution)/shard_map/moh/pallas_call | solution.py:395
  58.4 0.7 %copy.8 = bf16[192,1024]{1,0:T(8,128)(2,1)} copy(bf16[192,1024]{1,0:T(8,128)(2,1)S(1)} %moh.1) | data formatting | bytes 786432
